TPU v7x, 512 devices: a whole 4x8x8 slice. The times are simulated.
512 devices in a mesh: depth: 32 (over z_lo, y, core), row: 16 (over z_hi, x).
Axes of the slice: x: 4, y: 8, z: 8 (z_hi: 4, z_lo: 2; z = z_hi * 2 + z_lo), core: 2. Of those that a mesh axis runs over, the one named last changes fastest.
Arguments:
- input_cells: bfloat16 [128, 256, 128, 128], P('depth', 'row'), may hold values from -6 to 6
- first_weight: bfloat16 [3, 3, 3, 64, 128], P(None, None, None, None, 'depth'), may hold values from -0.15625 to 0.15625
- second_weight: bfloat16 [3, 3, 3, 128, 256], P(None, None, None, None, 'depth'), may hold values from -0.109375 to 0.109375
Outputs:
- encoded: bfloat16 [32, 64, 32, 512], P('depth', 'row')
All inputs are finite; a program needn't handle non-finite values.
Results may differ from a plain program's by a relative error of at most 0.0049.
Values may be sent and summed in bfloat16 or wider, within the bound.
No kernel may reach another device: no remote copies, remote signals or barrier semaphores. Data moves between devices by JAX's collectives and lax.ppermute only.
A program may use at most 64 MiB of HBM per device.

v0:
```python
import jax
import jax.numpy as jnp
from jax import lax
from jax.sharding import PartitionSpec as P


def from_behind(x, axis, by):
    count = lax.axis_size(axis)
    pairs = [(i, i + by) for i in range(count) if 0 <= i + by < count]
    return lax.ppermute(x, axis, pairs)


def stacked(weight, depth_tap, row_tap):
    kernel_taps = weight[depth_tap, row_tap]
    zeros_block = jnp.zeros_like(kernel_taps[0])
    upper_part = jnp.concatenate([kernel_taps[1], kernel_taps[2]], 0)
    lower_part = jnp.concatenate([zeros_block, kernel_taps[0]], 0)
    return jnp.concatenate([upper_part, lower_part], 1)


def convolve(extended, weight):
    planes = extended.shape[0] - 1
    row_count = extended.shape[1] - 1
    pair_count = extended.shape[2]
    features = extended.shape[3]
    out_width = weight.shape[4]
    running = jnp.zeros((planes // 2 * (row_count // 2) * pair_count, 2 * out_width), jnp.float32)
    for depth_tap in range(3):
        for row_tap in range(3):
            window = extended[depth_tap : depth_tap + planes : 2, row_tap : row_tap + row_count : 2]
            running = running + jnp.dot(
                window.reshape(-1, features),
                stacked(weight, depth_tap, row_tap),
                preferred_element_type=jnp.float32,
            )
    running = running.reshape(planes // 2, row_count // 2, pair_count, 2 * out_width)
    carried = jnp.pad(running[:, :, :-1, out_width:], ((0, 0), (0, 0), (1, 0), (0, 0)))
    return running[..., :out_width] + carried


def finish(field):
    activated = jnp.maximum(field, 0.0).astype(jnp.bfloat16)
    shape_now = activated.shape
    return activated.reshape(shape_now[0], shape_now[1], shape_now[2] // 2, 2 * shape_now[3])


def per_device(input_cells, first_weight, second_weight):
    first_full, second_full = (
        lax.all_gather(first_weight, "depth", axis=4, tiled=True),
        lax.all_gather(second_weight, "depth", axis=4, tiled=True),
    )
    below_plane = from_behind(input_cells[-1:], "depth", 1)
    with_plane = jnp.concatenate([below_plane, input_cells], 0)
    below_row = from_behind(with_plane[:, -1:], "row", 1)
    extended = jnp.concatenate([below_row, with_plane], 1)
    hidden = finish(convolve(extended, first_full))
    hidden_below = from_behind(hidden[-1:], "depth", 1)
    hidden_plus = jnp.concatenate([hidden_below, hidden], 0)
    hidden_rowrim = from_behind(hidden_plus[:, -1:], "row", 1)
    hidden_ext = jnp.concatenate([hidden_rowrim, hidden_plus], 1)
    summed = convolve(hidden_ext, second_full)
    return finish(summed)


def solution(mesh):
    return jax.shard_map(
        per_device,
        mesh=mesh,
        in_specs=(
            P("depth", "row", None, None),
            P(None, None, None, None, "depth"),
            P(None, None, None, None, "depth"),
        ),
        out_specs=P("depth", "row", None, None),
        check_vma=False,
    )
```

profile of v0, /device:TPU:320, one launch (start us, length us, event | category | flops | bytes accessed | tf_op | source)
XLA Modules:
  0.0 143.2 jit_solution(11971589362399876247)
XLA Ops:
  6.5 0.7 all-gather.2.cloned.1.call-update
  7.3 1.9 %slice.378 = bf16[1,16,128,128]{3,2,1,0:T(8,128)(2,1)} slice(bf16[4,16,128,128]{3,2,1,0:T(8,128)(2,1)} %param.3), slice={[3:4], [0:16], [0:128], [0:128]} | slice | bytes 1048576 | tf_op jit(solution)/shard_map/slice | solution.py:52
  9.2 1.9 %collective-permute-start = (bf16[1,16,128,128]{3,2,1,0:T(8,128)(2,1)}, bf16[1,16,128,128]{3,2,1,0:T(8,128)(2,1)}, u32[]{:S(2)}, u32[]{:S(2)}) collective-permute-start(bf16[1,16,128,128]{3,2,1,0:T(8,128)(2,1)} %slice.378), channel_id=1, source_target_pairs={{0,16},{16,32},{32,48},{48,64},{64,80},{80,96},{96,112},{112,128},... | collective-permute-start | bytes 1572872 | tf_op jit(solution)/shard_map/ppermute | solution.py:10
  11.1 0.8 copy.31
  11.9 37.9 %all_gather.6 = bf16[3,3,3,64,128]{3,2,1,0,4:T(4,128)(2,1)S(1)} all-gather(bf16[3,3,3,64,4]{3,2,1,0,4:T(4,128)(2,1)S(1)} %copy.31), channel_id=1, replica_groups=mesh['depth'=32,'row'=16] {'depth'}, dimensions={4}, use_global_device_ids=true | all-gather | bytes 456192 | tf_op jit(solution)/shard_map/all_gather | solution.py:49
  49.7 1.2 fusion.232
  50.9 2.0 %fusion.231 = (bf16[1,1,1,64,128]{3,2,1,0,4:T(2,128)(2,1)}, bf16[1,1,1,64,128]{3,2,1,0,4:T(2,128)(2,1)}, bf16[1,1,1,64,128]{3,2,1,0,4:T(2,128)(2,1)}, bf16[1,1,1...) fusion(bf16[3,3,3,64,128]{3,2,1,0,4:T(4,128)(2,1)S(1)} %all_gat, ...), kind=kLoop, calls=%fused_computation.265 | loop fusion | bytes 622592 | tf_op jit(solution)/shard_map/slice | solution.py:16
  52.9 1.2 fusion.230
  54.1 0.9 copy.93
  55.0 1.5 %copy.73 = bf16[1,1,1,64,128]{4,3,2,1,0:T(8,128)(2,1)} copy(bf16[1,1,1,64,128]{3,2,1,0,4:T(2,128)(2,1)} %get-tuple-element.61) | data formatting | bytes 32768
  56.6 1.5 %copy.72 = bf16[1,1,1,64,128]{4,3,2,1,0:T(8,128)(2,1)} copy(bf16[1,1,1,64,128]{3,2,1,0,4:T(2,128)(2,1)} %get-tuple-element.62) | data formatting | bytes 32768
  58.1 1.5 %copy.71 = bf16[1,1,1,64,128]{4,3,2,1,0:T(8,128)(2,1)} copy(bf16[1,1,1,64,128]{3,2,1,0,4:T(2,128)(2,1)} %get-tuple-element.63) | data formatting | bytes 32768
  59.6 1.5 %copy.70 = bf16[1,1,1,64,128]{4,3,2,1,0:T(8,128)(2,1)} copy(bf16[1,1,1,64,128]{3,2,1,0,4:T(2,128)(2,1)} %get-tuple-element.64) | data formatting | bytes 32768
  61.2 1.5 %copy.69 = bf16[1,1,1,64,128]{4,3,2,1,0:T(8,128)(2,1)} copy(bf16[1,1,1,64,128]{3,2,1,0,4:T(2,128)(2,1)} %get-tuple-element.65) | data formatting | bytes 32768
  62.7 1.5 %copy.68 = bf16[1,1,1,64,128]{4,3,2,1,0:T(8,128)(2,1)} copy(bf16[1,1,1,64,128]{3,2,1,0,4:T(2,128)(2,1)} %get-tuple-element.66) | data formatting | bytes 32768
  64.2 1.5 %copy.67 = bf16[1,1,1,64,128]{4,3,2,1,0:T(8,128)(2,1)} copy(bf16[1,1,1,64,128]{3,2,1,0,4:T(2,128)(2,1)} %get-tuple-element.67) | data formatting | bytes 32768
  65.7 1.5 %copy.91 = bf16[1,1,1,64,128]{4,3,2,1,0:T(8,128)(2,1)} copy(bf16[1,1,1,64,128]{3,2,1,0,4:T(2,128)(2,1)} %get-tuple-element.41) | data formatting | bytes 32768
  67.3 1.5 %copy.92 = bf16[1,1,1,64,128]{4,3,2,1,0:T(8,128)(2,1)} copy(bf16[1,1,1,64,128]{3,2,1,0,4:T(2,128)(2,1)} %get-tuple-element.42) | data formatting | bytes 32768
  68.8 1.5 %copy.90 = bf16[1,1,1,64,128]{4,3,2,1,0:T(8,128)(2,1)} copy(bf16[1,1,1,64,128]{3,2,1,0,4:T(2,128)(2,1)} %get-tuple-element.43) | data formatting | bytes 32768
  70.3 1.5 %copy.89 = bf16[1,1,1,64,128]{4,3,2,1,0:T(8,128)(2,1)} copy(bf16[1,1,1,64,128]{3,2,1,0,4:T(2,128)(2,1)} %get-tuple-element.44) | data formatting | bytes 32768
  71.9 1.5 %copy.88 = bf16[1,1,1,64,128]{4,3,2,1,0:T(8,128)(2,1)} copy(bf16[1,1,1,64,128]{3,2,1,0,4:T(2,128)(2,1)} %get-tuple-element.45) | data formatting | bytes 32768
  73.4 1.5 %copy.87 = bf16[1,1,1,64,128]{4,3,2,1,0:T(8,128)(2,1)} copy(bf16[1,1,1,64,128]{3,2,1,0,4:T(2,128)(2,1)} %get-tuple-element.46) | data formatting | bytes 32768
  74.9 1.5 %copy.86 = bf16[1,1,1,64,128]{4,3,2,1,0:T(8,128)(2,1)} copy(bf16[1,1,1,64,128]{3,2,1,0,4:T(2,128)(2,1)} %get-tuple-element.47) | data formatting | bytes 32768
  76.5 1.5 %copy.85 = bf16[1,1,1,64,128]{4,3,2,1,0:T(8,128)(2,1)} copy(bf16[1,1,1,64,128]{3,2,1,0,4:T(2,128)(2,1)} %get-tuple-element.48) | data formatting | bytes 32768
  78.0 1.5 %copy.84 = bf16[1,1,1,64,128]{4,3,2,1,0:T(8,128)(2,1)} copy(bf16[1,1,1,64,128]{3,2,1,0,4:T(2,128)(2,1)} %get-tuple-element.49) | data formatting | bytes 32768
  79.5 1.5 %copy.83 = bf16[1,1,1,64,128]{4,3,2,1,0:T(8,128)(2,1)} copy(bf16[1,1,1,64,128]{3,2,1,0,4:T(2,128)(2,1)} %get-tuple-element.50) | data formatting | bytes 32768
  81.1 1.5 %copy.82 = bf16[1,1,1,64,128]{4,3,2,1,0:T(8,128)(2,1)} copy(bf16[1,1,1,64,128]{3,2,1,0,4:T(2,128)(2,1)} %get-tuple-element.51) | data formatting | bytes 32768
  82.6 1.5 %copy.81 = bf16[1,1,1,64,128]{4,3,2,1,0:T(8,128)(2,1)} copy(bf16[1,1,1,64,128]{3,2,1,0,4:T(2,128)(2,1)} %get-tuple-element.52) | data formatting | bytes 32768
  84.1 1.5 %copy.80 = bf16[1,1,1,64,128]{4,3,2,1,0:T(8,128)(2,1)} copy(bf16[1,1,1,64,128]{3,2,1,0,4:T(2,128)(2,1)} %get-tuple-element.53) | data formatting | bytes 32768
  85.7 0.7 copy.79
  86.9 1.5 %convolution_bitcast_fusion.3 = f32[2048,256]{1,0:T(8,128)S(1)} fusion(bf16[2048,128]{1,0:T(8,128)(2,1)} %bitcast.146, bf16[64,128]{1,0:T(8,128)(2,1)} %bitcast.183, bf16[64,128]{1,0:T(8,128)(2,1)} %bitcast.184, bf16[64,128]{1,0:T(8,128)(2,1)} %bitcast.185), kind=kOutput, calls=%fused_computation.4 | convolution fusion | flops 134479872 | bytes 2670592 | tf_op jit(solution)/shard_map/dot_general | solution.py:31
  88.5 0.4 convolution_bitcast_fusion.1
  88.9 1.1 constant_dynamic-update-slice_fusion.1
  90.0 0.3 constant_dynamic-update-slice_fusion
  90.4 3.4 %collective-permute-start.1 = (bf16[5,1,128,128]{3,2,1,0:T(8,128)(2,1)S(1)}, bf16[5,1,128,128]{3,2,1,0:T(8,128)(2,1)S(1)}, u32[]{:S(2)}, u32[]{:S(2)}) collective-permute-start(bf16[5,1,128,128]{3,2,1,0:T(8,128)(2,1)S(1)} %slice.459), channel_id=1, source_target_pairs={{0,1},{1,2},{2,3},{3,4},{4,5},{5,6},{6,7},{7,8},{8,9},{9,10},{10,1... | collective-permute-start | bytes 491528 | tf_op jit(solution)/shard_map/ppermute | solution.py:10
  93.8 0.4 fusion.106
  94.3 0.4 fusion.103
  94.7 11.8 %collective-permute-done.1 = bf16[5,1,128,128]{3,2,1,0:T(8,128)(2,1)S(1)} collective-permute-done((bf16[5,1,128,128]{3,2,1,0:T(8,128)(2,1)S(1)}, bf16[5,1,128,128]{3,2,1,0:T(8,128)(2,1)S(1)}, u32[]{:S(2)}, u32[]{:S(2)}) %collective-permute-start.1) | collective-permute-done | bytes 163872 | tf_op jit(solution)/shard_map/ppermute | solution.py:10
  106.5 0.2 pad_maximum_fusion
  106.8 0.2 fusion.228
  107.0 0.5 copy-done.8
  107.5 0.4 fusion.4
  108.0 0.6 fusion.3
  108.7 0.4 fusion
  109.1 0.3 copy-done.5
  109.5 0.6 fusion.2
  110.2 0.4 fusion.1
  110.7 0.2 fusion.6
  111.0 1.9 %collective-permute-start.2 = (bf16[1,8,64,256]{3,2,1,0:T(8,128)(2,1)S(1)}, bf16[1,8,64,256]{3,2,1,0:T(8,128)(2,1)S(1)}, u32[]{:S(2)}, u32[]{:S(2)}) collective-permute-start(bf16[1,8,64,256]{3,2,1,0:T(8,128)(2,1)S(1)} %slice.419), channel_id=1, source_target_pairs={{0,16},{16,32},{32,48},{48,64},{64,80},{80,96},{96,112},{112,128},... | collective-permute-start | bytes 786440 | tf_op jit(solution)/shard_map/ppermute | solution.py:10
  112.9 0.2 reshape.185
  113.2 7.6 %collective-permute-done.2 = bf16[1,8,64,256]{3,2,1,0:T(8,128)(2,1)S(1)} collective-permute-done((bf16[1,8,64,256]{3,2,1,0:T(8,128)(2,1)S(1)}, bf16[1,8,64,256]{3,2,1,0:T(8,128)(2,1)S(1)}, u32[]{:S(2)}, u32[]{:S(2)}) %collective-permute-start.2) | collective-permute-done | bytes 262176 | tf_op jit(solution)/shard_map/ppermute | solution.py:10
  120.9 1.9 %collective-permute-start.3 = (bf16[3,1,64,256]{3,2,1,0:T(8,128)(2,1)S(1)}, bf16[3,1,64,256]{3,2,1,0:T(8,128)(2,1)S(1)}, u32[]{:S(2)}, u32[]{:S(2)}) collective-permute-start(bf16[3,1,64,256]{3,2,1,0:T(8,128)(2,1)S(1)} %slice.490), channel_id=1, source_target_pairs={{0,1},{1,2},{2,3},{3,4},{4,5},{5,6},{6,7},{7,8},{8,9},{9,10},{10,1... | collective-permute-start | bytes 294920 | tf_op jit(solution)/shard_map/ppermute | solution.py:10
  122.8 8.8 %collective-permute-done.3 = bf16[3,1,64,256]{3,2,1,0:T(8,128)(2,1)S(1)} collective-permute-done((bf16[3,1,64,256]{3,2,1,0:T(8,128)(2,1)S(1)}, bf16[3,1,64,256]{3,2,1,0:T(8,128)(2,1)S(1)}, u32[]{:S(2)}, u32[]{:S(2)}) %collective-permute-start.3) | collective-permute-done | bytes 98336 | tf_op jit(solution)/shard_map/ppermute | solution.py:10
  131.8 1.2 slice_bitcast_fusion.20
  133.0 0.2 fusion.19
  133.3 0.3 convolution_add_fusion.10
  133.7 0.3 convolution_add_fusion.9
  133.9 0.3 convolution_add_fusion.8
  134.2 0.3 convolution_add_fusion.7
  134.5 0.3 convolution_add_fusion.6
  134.7 0.3 convolution_add_fusion.5
  135.0 0.3 convolution_add_fusion.4
  135.3 0.3 convolution_add_fusion.3
  135.6 0.7 reshape.196
  (63 shorter events, 1.6 us)
Async XLA Ops:
  6.5 125.2 %all-gather.2.cloned.1.call-start = ((), (), s32[]{:S(2)}) async-start(), calls=%async_computation | async-start | bytes 1824768 | tf_op jit(solution)/shard_map/all_gather | solution.py:50
  9.2 79.7 %collective-permute-start = (bf16[1,16,128,128]{3,2,1,0:T(8,128)(2,1)}, bf16[1,16,128,128]{3,2,1,0:T(8,128)(2,1)}, u32[]{:S(2)}, u32[]{:S(2)}) collective-permute-start(bf16[1,16,128,128]{3,2,1,0:T(8,128)(2,1)} %slice.378), channel_id=1, source_target_pairs={{0,16},{16,32},{32,48},{48,64},{64,80},{80,96},{96,112},{112,128},... | collective-permute-start | bytes 1572872 | tf_op jit(solution)/shard_map/ppermute | solution.py:10
  11.9 41.0 %copy-start = (bf16[4,16,128,128]{3,2,1,0:T(8,128)(2,1)S(1)}, bf16[4,16,128,128]{3,2,1,0:T(8,128)(2,1)}, u32[]{:S(2)}) copy-start(bf16[4,16,128,128]{3,2,1,0:T(8,128)(2,1)} %param.3) | copy-start | bytes 6291460
  86.4 2.1 %copy-start.18 = (bf16[1,1,1,64,128]{4,3,2,1,0:T(8,128)(2,1)S(1)}, bf16[1,1,1,64,128]{4,3,2,1,0:T(8,128)(2,1)}, u32[]{:S(2)}) copy-start(bf16[1,1,1,64,128]{4,3,2,1,0:T(8,128)(2,1)} %copy.90) | copy-start | bytes 49156
  86.5 2.0 %copy-start.19 = (bf16[1,1,1,64,128]{4,3,2,1,0:T(8,128)(2,1)S(1)}, bf16[1,1,1,64,128]{4,3,2,1,0:T(8,128)(2,1)}, u32[]{:S(2)}) copy-start(bf16[1,1,1,64,128]{4,3,2,1,0:T(8,128)(2,1)} %copy.89) | copy-start | bytes 49156
  86.5 2.0 %copy-start.20 = (bf16[1,1,1,64,128]{4,3,2,1,0:T(8,128)(2,1)S(1)}, bf16[1,1,1,64,128]{4,3,2,1,0:T(8,128)(2,1)}, u32[]{:S(2)}) copy-start(bf16[1,1,1,64,128]{4,3,2,1,0:T(8,128)(2,1)} %copy.88) | copy-start | bytes 49156
  86.9 1.6 %copy-start.1 = (bf16[2,8,128,128]{3,2,1,0:T(8,128)(2,1)S(1)}, bf16[2,8,128,128]{3,2,1,0:T(8,128)(2,1)}, u32[]{:S(2)}) copy-start(bf16[2,8,128,128]{3,2,1,0:T(8,128)(2,1)} %get-tuple-element.13) | copy-start | bytes 1572868
  90.3 3.6 %copy-start.17 = (bf16[1,1,1,64,128]{4,3,2,1,0:T(8,128)(2,1)S(1)}, bf16[1,1,1,64,128]{4,3,2,1,0:T(8,128)(2,1)}, u32[]{:S(2)}) copy-start(bf16[1,1,1,64,128]{4,3,2,1,0:T(8,128)(2,1)} %copy.73) | copy-start | bytes 49156
  90.3 3.9 %copy-start.14 = (bf16[1,1,1,64,128]{4,3,2,1,0:T(8,128)(2,1)S(1)}, bf16[1,1,1,64,128]{4,3,2,1,0:T(8,128)(2,1)}, u32[]{:S(2)}) copy-start(bf16[1,1,1,64,128]{4,3,2,1,0:T(8,128)(2,1)} %copy.72) | copy-start | bytes 49156
  90.3 3.9 %copy-start.15 = (bf16[1,1,1,64,128]{4,3,2,1,0:T(8,128)(2,1)S(1)}, bf16[1,1,1,64,128]{4,3,2,1,0:T(8,128)(2,1)}, u32[]{:S(2)}) copy-start(bf16[1,1,1,64,128]{4,3,2,1,0:T(8,128)(2,1)} %copy.71) | copy-start | bytes 49156
  90.3 3.9 %copy-start.16 = (bf16[1,1,1,64,128]{4,3,2,1,0:T(8,128)(2,1)S(1)}, bf16[1,1,1,64,128]{4,3,2,1,0:T(8,128)(2,1)}, u32[]{:S(2)}) copy-start(bf16[1,1,1,64,128]{4,3,2,1,0:T(8,128)(2,1)} %copy.70) | copy-start | bytes 49156
  90.4 16.1 %collective-permute-start.1 = (bf16[5,1,128,128]{3,2,1,0:T(8,128)(2,1)S(1)}, bf16[5,1,128,128]{3,2,1,0:T(8,128)(2,1)S(1)}, u32[]{:S(2)}, u32[]{:S(2)}) collective-permute-start(bf16[5,1,128,128]{3,2,1,0:T(8,128)(2,1)S(1)} %slice.459), channel_id=1, source_target_pairs={{0,1},{1,2},{2,3},{3,4},{4,5},{5,6},{6,7},{7,8},{8,9},{9,10},{10,1... | collective-permute-start | bytes 491528 | tf_op jit(solution)/shard_map/ppermute | solution.py:10
  106.8 0.7 copy-start.8
  106.8 0.7 copy-start.9
  106.8 0.7 copy-start.10
  107.9 0.7 copy-start.11
  108.0 0.7 copy-start.12
  108.0 0.7 copy-start.13
  108.7 0.7 copy-start.5
  108.7 0.7 copy-start.6
  108.7 0.7 copy-start.7
  109.4 0.7 copy-start.3
  109.4 0.7 copy-start.4
  111.0 9.8 %collective-permute-start.2 = (bf16[1,8,64,256]{3,2,1,0:T(8,128)(2,1)S(1)}, bf16[1,8,64,256]{3,2,1,0:T(8,128)(2,1)S(1)}, u32[]{:S(2)}, u32[]{:S(2)}) collective-permute-start(bf16[1,8,64,256]{3,2,1,0:T(8,128)(2,1)S(1)} %slice.419), channel_id=1, source_target_pairs={{0,16},{16,32},{32,48},{48,64},{64,80},{80,96},{96,112},{112,128},... | collective-permute-start | bytes 786440 | tf_op jit(solution)/shard_map/ppermute | solution.py:10
  120.9 10.7 %collective-permute-start.3 = (bf16[3,1,64,256]{3,2,1,0:T(8,128)(2,1)S(1)}, bf16[3,1,64,256]{3,2,1,0:T(8,128)(2,1)S(1)}, u32[]{:S(2)}, u32[]{:S(2)}) collective-permute-start(bf16[3,1,64,256]{3,2,1,0:T(8,128)(2,1)S(1)} %slice.490), channel_id=1, source_target_pairs={{0,1},{1,2},{2,3},{3,4},{4,5},{5,6},{6,7},{7,8},{8,9},{9,10},{10,1... | collective-permute-start | bytes 294920 | tf_op jit(solution)/shard_map/ppermute | solution.py:10
  131.8 1.8 %copy-start.2 = (bf16[3,3,3,128,256]{3,4,2,1,0:T(8,128)(2,1)S(1)}, bf16[3,3,3,128,256]{3,4,2,1,0:T(8,128)(2,1)}, u32[]{:S(2)}) copy-start(bf16[3,3,3,128,256]{3,4,2,1,0:T(8,128)(2,1)} %all-gather.2.cloned.1.call-done) | copy-start | bytes 5308420
Sparse Core Ops, SparseCore 0:
  9.4 68.9 all-gather.1
where the time goes:
time: 145 us; the launch traced here: 143 us
  local copies, waits for them, and re-layouts  45.2 us (31%)
  blocking collectives  37.9 us (26%)
  waiting for transfers between devices  29 us (20%)
  between operations  14 us (10%)
  starting transfers between devices  9.12 us (6%)
  matrix products  7.49 us (5%)
    all_gather x1, blocking collectives, per_device(): lax.all_gather(first_weight, 'depth', axis=4, tiled=True)  37.9 us
    unnamed x72, local copies, waits for them, and re-layouts  35.8 us
    ppermute x4, waiting for transfers between devices, from_behind(): return lax.ppermute(x, axis, pairs)  28.3 us
    ppermute x4, starting transfers between devices, from_behind(): return lax.ppermute(x, axis, pairs)  9.12 us
    dot_general x18, matrix products, convolve(): jnp.dot(window.reshape(-1, features), stacked(weight, depth_tap, row_tap)...  7.49 us
  transfers between devices with their start and end apart: 5, of which 3 were waited for; matrix products, arithmetic and copies ran while one was open for 33% of the time, Pallas kernels for 0%

commit v1 on v0

v1 whole, which is shorter than its diff:
```python
import jax
import jax.numpy as jnp
from jax import lax
from jax.experimental import pallas as pl
from jax.experimental.pallas import tpu as pltpu
from jax.sharding import PartitionSpec as P

F32 = jnp.float32
BF16 = jnp.bfloat16
VMEM = pltpu.VMEM
SPEC = pl.BlockSpec(memory_space=pltpu.VMEM)


def dot_t(a, b):
    return lax.dot_general(a, b, (((1,), (1,)), ((), ())), preferred_element_type=F32)


def first_kernel(x_ref, plane_ref, rim_ref, corner_ref, g_ref, h0_ref, h1_ref, stage, rows_up, weights, up, low):
    lanes = lax.broadcasted_iota(jnp.int32, (128, 128), 1)
    right = lanes >= 64
    for tile in range(7):
        stage[...] = g_ref[tile // 4, :, tile % 4].astype(F32).reshape(256, 128)
        for r in range(8):
            rows_up[r // 4, pl.ds(r % 4, 32, stride=4)] = stage[pl.ds(r, 32, stride=8)]
        for half in range(2):
            group = 2 * tile + half
            block = rows_up[half]
            if group < 9:
                weights[group, 0:128] = block.astype(BF16)
            else:
                tap = 2 * (group - 9)
                weights[tap, 128:256] = jnp.where(right, pltpu.roll(block, 64, 1), 0.0).astype(BF16)
                if tap + 1 < 9:
                    weights[tap + 1, 128:256] = jnp.where(right, block, 0.0).astype(BF16)

    def window(plane, j):
        if plane == 0:
            x, rim = plane_ref[0], corner_ref[0]
        else:
            x, rim = x_ref[plane - 1], rim_ref[plane - 1]
        x = x.reshape(8, 2, 128, 128)
        if j == 0:
            parts = [rim[0:1], rim[2:3], x[0:7, 1]]
        elif j == 1:
            parts = [rim[1:2], x[:, 0]]
        else:
            parts = [rim[2:3], x[:, 1]]
        return jnp.concatenate(parts, 0).reshape(1152, 128)

    for a in range(2):
        for tap in range(9):
            i, j = divmod(tap, 3)
            both = dot_t(window(2 * a + i, j), weights[tap]).reshape(9, 128, 256)
            if tap == 0:
                up[...] = both[:, :, :128]
                low[:, 8:136] = both[:, :, 128:]
                low[:, 0:8] = jnp.zeros((9, 8, 128), F32)
            else:
                up[...] += both[:, :, :128]
                low[:, 8:136] += both[:, :, 128:]
        out = (h0_ref, h1_ref)[a]
        for b in range(9):
            even = up[b, pl.ds(0, 64, stride=2)] + low[b, pl.ds(7, 64, stride=2)]
            odd = up[b, pl.ds(1, 64, stride=2)] + low[b, pl.ds(8, 64, stride=2)]
            out[b, :, 0:128] = jnp.maximum(even, 0.0).astype(BF16)
            out[b, :, 128:256] = jnp.maximum(odd, 0.0).astype(BF16)


def first_layer(x, plane, rim, corner, g):
    shape = jax.ShapeDtypeStruct((9, 64, 256), BF16)
    return pl.pallas_call(
        first_kernel,
        out_shape=(shape, shape),
        in_specs=[SPEC] * 5,
        out_specs=(SPEC, SPEC),
        scratch_shapes=[
            VMEM((256, 128), F32),
            VMEM((2, 128, 128), F32),
            VMEM((9, 256, 128), BF16),
            VMEM((9, 128, 128), F32),
            VMEM((9, 136, 128), F32),
        ],
        compiler_params=pltpu.CompilerParams(vmem_limit_bytes=40 * 2**20),
        cost_estimate=pl.CostEstimate(flops=2 * 2304 * 1152 * 256, bytes_accessed=4 * 2**20, transcendentals=0),
        name="first_layer",
    )(x, plane, rim, corner, g)


def second_kernel(core_ref, hm_ref, h0_ref, h1_ref, g_ref, mine_ref, theirs_ref, out_ref, up, low):
    planes = (hm_ref, h0_ref, h1_ref)

    def weight(block):
        return block.astype(F32).reshape(256, 128).astype(BF16)

    def body(first_ref, last_ref):
        low[:, :, 0:8] = jnp.zeros((2, 4, 8, 128), F32)

        def tap_of(t):
            if t < 13:
                return weight(first_ref[:, t])
            if t == 13:
                return weight(g_ref[1, :, 3])
            return weight(last_ref[:, t - 14])

        for tap in range(9):
            i, j = divmod(tap, 3)
            cells = jnp.concatenate([planes[i][j + 2 * b] for b in range(4)], 0)
            k0, k1, k2 = (tap_of(3 * tap + k) for k in range(3))
            u = dot_t(cells, jnp.concatenate([k1, k2], 1))
            v = dot_t(cells[:, 128:], k0).reshape(4, 64, 256)
            for n in range(2):
                lanes = slice(128 * n, 128 * n + 128)
                if tap == 0:
                    up[n] = u[:, lanes]
                    low[n, :, 8:72] = v[:, :, lanes]
                else:
                    up[n] += u[:, lanes]
                    low[n, :, 8:72] += v[:, :, lanes]

    @pl.when(core_ref[0] == 0)
    def _():
        body(mine_ref, theirs_ref)

    @pl.when(core_ref[0] != 0)
    def _():
        body(theirs_ref, mine_ref)

    for b in range(4):
        for n in range(2):
            even = up[n, pl.ds(64 * b, 32, stride=2)] + low[n, b, pl.ds(7, 32, stride=2)]
            odd = up[n, pl.ds(64 * b + 1, 32, stride=2)] + low[n, b, pl.ds(8, 32, stride=2)]
            out_ref[0, b, :, 128 * n : 128 * n + 128] = jnp.maximum(even, 0.0).astype(BF16)
            out_ref[0, b, :, 256 + 128 * n : 384 + 128 * n] = jnp.maximum(odd, 0.0).astype(BF16)


def second_layer(core, hm, h0, h1, g, mine, theirs):
    return pl.pallas_call(
        second_kernel,
        out_shape=jax.ShapeDtypeStruct((1, 4, 32, 512), BF16),
        in_specs=[pl.BlockSpec(memory_space=pltpu.SMEM)] + [SPEC] * 6,
        out_specs=SPEC,
        scratch_shapes=[VMEM((2, 256, 128), F32), VMEM((2, 4, 72, 128), F32)],
        compiler_params=pltpu.CompilerParams(vmem_limit_bytes=40 * 2**20),
        cost_estimate=pl.CostEstimate(flops=2 * 256 * 3456 * 256, bytes_accessed=3 * 2**20, transcendentals=0),
        name="second_layer",
    )(core, hm, h0, h1, g, mine, theirs)


def packed(first, second):
    taps = first.transpose(0, 1, 2, 4, 3).reshape(9, 3, 4, 64)
    pair = jnp.concatenate([taps[:, 1], taps[:, 2]], -1)
    single = jnp.pad(taps[:, 0], ((0, 1), (0, 0), (0, 0))).reshape(5, 2, 4, 64)
    single = jnp.concatenate([single[:, 0], single[:, 1]], -1)
    w1 = jnp.concatenate([pair, single], 0).reshape(7, 8, 128)
    w2 = second.transpose(0, 1, 2, 4, 3).reshape(27, 8, 128)
    half0 = jnp.concatenate([w1[:4], w2[:13]], 0)
    half1 = jnp.concatenate([w1[4:], w2[13:]], 0)
    return jnp.stack([half0, half1])


def shift_by_one(x, axes, counts):
    if len(axes) == 1:
        pairs = [(i, i + 1) for i in range(counts[0] - 1)]
        return lax.ppermute(x, axes[0], pairs)
    n, m = counts
    pairs = [(i * m + j, (i + 1) * m + j + 1) for i in range(n - 1) for j in range(m - 1)]
    return lax.ppermute(x, axes, pairs)


def per_device(x, first_weight, second_weight):
    nd, nr = lax.axis_size("depth"), lax.axis_size("row")
    halves = packed(first_weight, second_weight)
    send = jnp.broadcast_to(halves[None], (nd // 2, 2, 17, 8, 128)).reshape(nd, 17, 8, 128)
    got = lax.all_to_all(send, "depth", 0, 0, tiled=False)

    rim = shift_by_one(x[:, 13:], ("row",), (nr,))
    plane = shift_by_one(x[3:], ("depth",), (nd,))
    corner = shift_by_one(x[3:, 13:], ("depth", "row"), (nd, nr))

    got, rim, plane, corner = lax.optimization_barrier((got, rim, plane, corner))

    partners = [(i, i ^ 1) for i in range(nd)]
    groups = [[i, i + 1] for i in range(0, nd, 2)]
    g = lax.all_gather(got[:, :4], "depth", axis_index_groups=groups)
    mine = got[:, 4:]
    theirs = lax.ppermute(mine, "depth", partners)

    h0, h1 = first_layer(x, plane, rim, corner, g)
    hm = shift_by_one(h1, ("depth",), (nd,))
    core = (lax.axis_index("depth") % 2).astype(jnp.int32).reshape(1)
    return second_layer(core, hm, h0, h1, g, mine, theirs)


def solution(mesh):
    return jax.shard_map(
        per_device,
        mesh=mesh,
        in_specs=(
            P("depth", "row", None, None),
            P(None, None, None, None, "depth"),
            P(None, None, None, None, "depth"),
        ),
        out_specs=P("depth", "row", None, None),
        check_vma=False,
    )
```

time: 145 us -> 77.9 us (0.54)
  the two profiles are of different devices: /device:TPU:320 before, /device:TPU:392 now
where the time goes in v1:
time: 77.9 us; the launch traced here: 77.3 us
  waiting for transfers between devices  37.3 us (48%)
  starting transfers between devices  23.6 us (30%)
  local copies, waits for them, and re-layouts  8.86 us (11%)
  Pallas kernels  4.87 us (6%)
  blocking collectives  2.33 us (3%)
    ppermute x1, waiting for transfers between devices, shift_by_one(): return lax.ppermute(x, axes, pairs)  22.7 us
    ppermute x3, waiting for transfers between devices, shift_by_one(): return lax.ppermute(x, axes[0], pairs)  14.6 us
    all_to_all x1, starting transfers between devices, per_device(): got = lax.all_to_all(send, 'depth', 0, 0, tiled=False)  8.61 us
    ppermute x3, starting transfers between devices, shift_by_one(): return lax.ppermute(x, axes[0], pairs)  7.73 us
    ppermute x1, starting transfers between devices, shift_by_one(): return lax.ppermute(x, axes, pairs)  4.14 us
    pallas_call x1, Pallas kernels, first_layer(): pl.pallas_call(first_kernel, out_shape=(shape, shape), in_specs=[SPEC] *...  3.38 us
    ppermute x1, starting transfers between devices, per_device(): theirs = lax.ppermute(mine, 'depth', partners)  3.14 us
    unnamed x6, local copies, waits for them, and re-layouts  2.36 us
  transfers between devices with their start and end apart: 6, of which 3 were waited for; matrix products, arithmetic and copies ran while one was open for 4% of the time, Pallas kernels for 4%

profile of v1, /device:TPU:392, one launch (start us, length us, event | category | flops | bytes accessed | tf_op | source)
XLA Modules:
  0.0 77.3 jit_solution(18119536748293267668)
XLA Ops:
  0.0 0.7 slice.67
  0.7 0.8 slice.71
  1.5 0.7 slice_bitcast_fusion.2
  2.3 0.1 pad_maximum_fusion.1
  2.4 0.1 fusion
  2.5 1.1 %broadcast_in_dim.2 = bf16[16,2,17,8,128]{4,3,2,1,0:T(8,128)(2,1)} broadcast(bf16[2,17,8,128]{3,2,1,0:T(8,128)(2,1)S(1)} %pad_maximum_fusion), dimensions={1,2,3,4} | broadcast | bytes 1183744 | tf_op jit(solution)/shard_map/broadcast_in_dim | solution.py:173
  3.6 8.6 %all-to-all-start = ((bf16[32,17,8,128]{3,2,1,0:T(8,128)(2,1)}), bf16[32,17,8,128]{3,2,1,0:T(8,128)(2,1)S(1)}, u32[]{:S(2)}, u32[]{:S(2)}) async-start(bf16[32,17,8,128]{3,2,1,0:T(8,128)(2,1)} %bitcast.17), calls=%async_computation | async-start | bytes 2228224 | tf_op jit(solution)/shard_map/all_to_all | solution.py:174
  12.2 1.1 %slice.61 = bf16[1,16,128,128]{3,2,1,0:T(8,128)(2,1)S(1)} slice(bf16[4,16,128,128]{3,2,1,0:T(8,128)(2,1)} %x_ref.1), slice={[3:4], [0:16], [0:128], [0:128]} | slice | bytes 1048576 | tf_op jit(solution)/shard_map/slice | solution.py:177
  13.3 2.1 %collective-permute-start.1 = (bf16[1,16,128,128]{3,2,1,0:T(8,128)(2,1)S(1)}, bf16[1,16,128,128]{3,2,1,0:T(8,128)(2,1)S(1)}, u32[]{:S(2)}, u32[]{:S(2)}) collective-permute-start(bf16[1,16,128,128]{3,2,1,0:T(8,128)(2,1)S(1)} %slice.61), channel_id=1, source_target_pairs={{0,16},{16,32},{32,48},{48,64},{64,80},{80,96},{96,112},{112,128},... | collective-permute-start | bytes 1572872 | tf_op jit(solution)/shard_map/ppermute | solution.py:164
  15.4 1.0 %slice.60 = bf16[4,3,128,128]{3,2,1,0:T(8,128)(2,1)S(1)} slice(bf16[4,16,128,128]{3,2,1,0:T(8,128)(2,1)} %x_ref.1), slice={[0:4], [13:16], [0:128], [0:128]} | slice | bytes 786432 | tf_op jit(solution)/shard_map/slice | solution.py:176
  16.4 3.4 %collective-permute-start = (bf16[4,3,128,128]{3,2,1,0:T(8,128)(2,1)S(1)}, bf16[4,3,128,128]{3,2,1,0:T(8,128)(2,1)S(1)}, u32[]{:S(2)}, u32[]{:S(2)}) collective-permute-start(bf16[4,3,128,128]{3,2,1,0:T(8,128)(2,1)S(1)} %slice.60), channel_id=1, source_target_pairs={{0,1},{1,2},{2,3},{3,4},{4,5},{5,6},{6,7},{7,8},{8,9},{9,10},{10,1... | collective-permute-start | bytes 1179656 | tf_op jit(solution)/shard_map/ppermute | solution.py:164
  19.8 0.9 %slice.62 = bf16[1,3,128,128]{3,2,1,0:T(8,128)(2,1)S(1)} slice(bf16[4,16,128,128]{3,2,1,0:T(8,128)(2,1)} %x_ref.1), slice={[3:4], [13:16], [0:128], [0:128]} | slice | bytes 196608 | tf_op jit(solution)/shard_map/slice | solution.py:178
  20.7 4.1 %collective-permute-start.2 = (bf16[1,3,128,128]{3,2,1,0:T(8,128)(2,1)S(1)}, bf16[1,3,128,128]{3,2,1,0:T(8,128)(2,1)S(1)}, u32[]{:S(2)}, u32[]{:S(2)}) collective-permute-start(bf16[1,3,128,128]{3,2,1,0:T(8,128)(2,1)S(1)} %slice.62), channel_id=1, source_target_pairs={{0,17},{1,18},{2,19},{3,20},{4,21},{5,22},{6,23},{7,24},{8,25},{9,... | collective-permute-start | bytes 294920 | tf_op jit(solution)/shard_map/ppermute | solution.py:167
  24.9 22.7 %collective-permute-done.2.corner_ref = bf16[1,3,128,128]{3,2,1,0:T(8,128)(2,1)S(1)} collective-permute-done((bf16[1,3,128,128]{3,2,1,0:T(8,128)(2,1)S(1)}, bf16[1,3,128,128]{3,2,1,0:T(8,128)(2,1)S(1)}, u32[]{:S(2)}, u32[]{:S(2)}) %collective-permute-start.2) | collective-permute-done | bytes 98336 | tf_op jit(solution)/shard_map/ppermute | solution.py:167
  47.6 4.9 %collective-permute-done.rim_ref = bf16[4,3,128,128]{3,2,1,0:T(8,128)(2,1)S(1)} collective-permute-done((bf16[4,3,128,128]{3,2,1,0:T(8,128)(2,1)S(1)}, bf16[4,3,128,128]{3,2,1,0:T(8,128)(2,1)S(1)}, u32[]{:S(2)}, u32[]{:S(2)}) %collective-permute-start) | collective-permute-done | bytes 393248 | tf_op jit(solution)/shard_map/ppermute | solution.py:164
  52.5 0.0 copy-start.1
  52.5 0.8 copy-done.1
  53.3 0.0 collective-permute-done.1.plane_ref
  53.3 0.0 all-to-all-done
  53.3 0.0 copy-start.2
  53.3 0.1 slice.64.mine_ref
  53.4 3.1 %collective-permute-start.4 = (bf16[32,13,8,128]{3,2,1,0:T(8,128)(2,1)S(1)}, bf16[32,13,8,128]{3,2,1,0:T(8,128)(2,1)S(1)}, u32[]{:S(2)}, u32[]{:S(2)}) collective-permute-start(bf16[32,13,8,128]{3,2,1,0:T(8,128)(2,1)S(1)} %slice.64.mine_ref), channel_id=1, source_target_pairs={{0,16},{16,0},{32,48},{48,32},{64,80},{80,64},{96,112},{112,96},{1... | collective-permute-start | bytes 2555912 | tf_op jit(solution)/shard_map/ppermute | solution.py:186
  56.6 2.3 %all-gather = bf16[64,4,8,128]{3,2,1,0:T(8,128)(2,1)S(1)} all-gather(bf16[32,4,8,128]{3,2,1,0:T(8,128)(2,1)S(1)} %slice.63), channel_id=2, replica_groups={{0,16},{32,48},{64,80},{96,112},{128,144},{160,176},{192,208},{224,240}..., dimensions={0}, use_global_device_ids=true | all-gather | bytes 786432 | tf_op jit(solution)/shard_map/all_gather | solution.py:184
  58.9 0.0 copy-done.2
  58.9 0.0 copy-start
  58.9 1.6 %copy-done = bf16[4,16,128,128]{3,2,1,0:T(8,128)(2,1)S(1)} copy-done((bf16[4,16,128,128]{3,2,1,0:T(8,128)(2,1)S(1)}, bf16[4,16,128,128]{3,2,1,0:T(8,128)(2,1)}, u32[]{:S(2)}) %copy-start) | copy-done | bytes 2097176
  60.5 3.4 %first_layer.1 = (bf16[9,64,256]{2,1,0:T(8,128)(2,1)S(1)}, bf16[9,64,256]{2,1,0:T(8,128)(2,1)S(1)}) custom-call(bf16[4,16,128,128]{3,2,1,0:T(8,128)(2,1)S(1)} %copy-done, bf16[1,16,128,128]{3,2,1,0:T(8,128)(2,1)S(1)} %collective-permute-done.1.plane_ref, bf16[4,3,128,128]{3,2,1,0:T(8,128)(2,1)S(1)} %copy-done.2, ...), custom_call_target="tpu_custom_call" | custom-call | flops 1358954496 | bytes 4194304 | tf_op jit(solution)/shard_map/first_layer/pallas_call | solution.py:71
  63.9 2.3 %collective-permute-start.3 = (bf16[9,64,256]{2,1,0:T(8,128)(2,1)S(1)}, bf16[9,64,256]{2,1,0:T(8,128)(2,1)S(1)}, u32[]{:S(2)}, u32[]{:S(2)}) collective-permute-start(bf16[9,64,256]{2,1,0:T(8,128)(2,1)S(1)} %get-tuple-element.15.h1_ref), channel_id=1, source_target_pairs={{0,16},{16,32},{32,48},{48,64},{64,80},{80,96},{96,112},{112,128},... | collective-permute-start | bytes 884744 | tf_op jit(solution)/shard_map/ppermute | solution.py:164
  66.2 9.6 %collective-permute-done.3.hm_ref = bf16[9,64,256]{2,1,0:T(8,128)(2,1)S(1)} collective-permute-done((bf16[9,64,256]{2,1,0:T(8,128)(2,1)S(1)}, bf16[9,64,256]{2,1,0:T(8,128)(2,1)S(1)}, u32[]{:S(2)}, u32[]{:S(2)}) %collective-permute-start.3) | collective-permute-done | bytes 294944 | tf_op jit(solution)/shard_map/ppermute | solution.py:164
  75.8 0.0 collective-permute-done.4.theirs_ref
  75.8 1.5 %second_layer.1 = bf16[1,4,32,512]{3,2,1,0:T(8,128)(2,1)} custom-call(s32[1]{0:T(128)} %bitcast.core_ref, bf16[9,64,256]{2,1,0:T(8,128)(2,1)S(1)} %collective-permute-done.3.hm_ref, bf16[9,64,256]{2,1,0:T(8,128)(2,1)S(1)} %get-tuple-element.16.h0_ref, bf16[9,64,256]{2,1,0:T(8,128)(2,1)S(1)} %get-tuple-element.15.h1_ref, ...), custom_call_target="tpu_custom_call" | custom-call | flops 452984832 | bytes 3145728 | tf_op jit(solution)/shard_map/second_layer/pallas_call | solution.py:137
  (5 shorter events, 0.1 us)
Async XLA Ops:
  3.6 49.7 %all-to-all-start = ((bf16[32,17,8,128]{3,2,1,0:T(8,128)(2,1)}), bf16[32,17,8,128]{3,2,1,0:T(8,128)(2,1)S(1)}, u32[]{:S(2)}, u32[]{:S(2)}) async-start(bf16[32,17,8,128]{3,2,1,0:T(8,128)(2,1)} %bitcast.17), calls=%async_computation | async-start | bytes 2228224 | tf_op jit(solution)/shard_map/all_to_all | solution.py:174
  13.3 40.0 %collective-permute-start.1 = (bf16[1,16,128,128]{3,2,1,0:T(8,128)(2,1)S(1)}, bf16[1,16,128,128]{3,2,1,0:T(8,128)(2,1)S(1)}, u32[]{:S(2)}, u32[]{:S(2)}) collective-permute-start(bf16[1,16,128,128]{3,2,1,0:T(8,128)(2,1)S(1)} %slice.61), channel_id=1, source_target_pairs={{0,16},{16,32},{32,48},{48,64},{64,80},{80,96},{96,112},{112,128},... | collective-permute-start | bytes 1572872 | tf_op jit(solution)/shard_map/ppermute | solution.py:164
  16.4 36.1 %collective-permute-start = (bf16[4,3,128,128]{3,2,1,0:T(8,128)(2,1)S(1)}, bf16[4,3,128,128]{3,2,1,0:T(8,128)(2,1)S(1)}, u32[]{:S(2)}, u32[]{:S(2)}) collective-permute-start(bf16[4,3,128,128]{3,2,1,0:T(8,128)(2,1)S(1)} %slice.60), channel_id=1, source_target_pairs={{0,1},{1,2},{2,3},{3,4},{4,5},{5,6},{6,7},{7,8},{8,9},{9,10},{10,1... | collective-permute-start | bytes 1179656 | tf_op jit(solution)/shard_map/ppermute | solution.py:164
  20.7 26.9 %collective-permute-start.2 = (bf16[1,3,128,128]{3,2,1,0:T(8,128)(2,1)S(1)}, bf16[1,3,128,128]{3,2,1,0:T(8,128)(2,1)S(1)}, u32[]{:S(2)}, u32[]{:S(2)}) collective-permute-start(bf16[1,3,128,128]{3,2,1,0:T(8,128)(2,1)S(1)} %slice.62), channel_id=1, source_target_pairs={{0,17},{1,18},{2,19},{3,20},{4,21},{5,22},{6,23},{7,24},{8,25},{9,... | collective-permute-start | bytes 294920 | tf_op jit(solution)/shard_map/ppermute | solution.py:167
  52.5 0.8 copy-start.1
  53.3 5.6 %copy-start.2 = (bf16[4,3,128,128]{3,2,1,0:T(8,128)(2,1)S(1)}, bf16[4,3,128,128]{3,2,1,0:T(8,128)(2,1)}, u32[]{:S(2)}) copy-start(bf16[4,3,128,128]{3,2,1,0:T(8,128)(2,1)} %copy-done.1) | copy-start | bytes 1179652
  53.4 22.4 %collective-permute-start.4 = (bf16[32,13,8,128]{3,2,1,0:T(8,128)(2,1)S(1)}, bf16[32,13,8,128]{3,2,1,0:T(8,128)(2,1)S(1)}, u32[]{:S(2)}, u32[]{:S(2)}) collective-permute-start(bf16[32,13,8,128]{3,2,1,0:T(8,128)(2,1)S(1)} %slice.64.mine_ref), channel_id=1, source_target_pairs={{0,16},{16,0},{32,48},{48,32},{64,80},{80,64},{96,112},{112,96},{1... | collective-permute-start | bytes 2555912 | tf_op jit(solution)/shard_map/ppermute | solution.py:186
  58.9 1.6 %copy-start = (bf16[4,16,128,128]{3,2,1,0:T(8,128)(2,1)S(1)}, bf16[4,16,128,128]{3,2,1,0:T(8,128)(2,1)}, u32[]{:S(2)}) copy-start(bf16[4,16,128,128]{3,2,1,0:T(8,128)(2,1)} %x_ref.1) | copy-start | bytes 6291460
  63.9 11.9 %collective-permute-start.3 = (bf16[9,64,256]{2,1,0:T(8,128)(2,1)S(1)}, bf16[9,64,256]{2,1,0:T(8,128)(2,1)S(1)}, u32[]{:S(2)}, u32[]{:S(2)}) collective-permute-start(bf16[9,64,256]{2,1,0:T(8,128)(2,1)S(1)} %get-tuple-element.15.h1_ref), channel_id=1, source_target_pairs={{0,16},{16,32},{32,48},{48,64},{64,80},{80,96},{96,112},{112,128},... | collective-permute-start | bytes 884744 | tf_op jit(solution)/shard_map/ppermute | solution.py:164

commit v2 on v1

v2 whole, which is shorter than its diff:
```python
import jax
import jax.numpy as jnp
from jax import lax
from jax.experimental import pallas as pl
from jax.experimental.pallas import tpu as pltpu
from jax.sharding import PartitionSpec as P

F32 = jnp.float32
BF16 = jnp.bfloat16
VMEM = pltpu.VMEM
SPEC = pl.BlockSpec(memory_space=pltpu.VMEM)


def dot_t(a, b):
    return lax.dot_general(a, b, (((1,), (1,)), ((), ())), preferred_element_type=F32)


def first_kernel(x_ref, edge_ref, rim_ref, mine_ref, theirs_ref, seen_ref, h0_ref, h1_ref, rows_ref, stage, rows_up, weights, up, low):
    lanes = lax.broadcasted_iota(jnp.int32, (128, 128), 1)
    right = lanes >= 64
    core = lax.axis_index("depth") & 1

    def unpack(lower_ref, upper_ref):
        for tile in range(7):
            stage[...] = (lower_ref, upper_ref)[tile // 4][:, tile % 4].astype(F32).reshape(256, 128)
            for r in range(8):
                rows_up[r // 4, pl.ds(r % 4, 32, stride=4)] = stage[pl.ds(r, 32, stride=8)]
            for half in range(2):
                group = 2 * tile + half
                block = rows_up[half]
                if group < 9:
                    weights[group, 0:128] = block.astype(BF16)
                else:
                    tap = 2 * (group - 9)
                    weights[tap, 128:256] = jnp.where(right, pltpu.roll(block, 64, 1), 0.0).astype(BF16)
                    if tap + 1 < 9:
                        weights[tap + 1, 128:256] = jnp.where(right, block, 0.0).astype(BF16)

    @pl.when(core == 0)
    def _():
        unpack(mine_ref, theirs_ref)

    @pl.when(core != 0)
    def _():
        unpack(theirs_ref, mine_ref)

    def window(plane, j):
        x = edge_ref[0] if plane == 0 else x_ref[plane - 1]
        x = x.reshape(8, 2, 128, 128)
        if j == 0:
            x = jnp.concatenate([rim_ref[plane], x[0:7, 1]], 0)
        else:
            x = x[:, j - 1]
        return x.reshape(1024, 128)

    for a in range(2):
        for tap in range(9):
            i, j = divmod(tap, 3)
            both = dot_t(window(2 * a + i, j), weights[tap]).reshape(8, 128, 256)
            if tap == 0:
                up[...] = both[:, :, :128]
                low[:, 8:136] = both[:, :, 128:]
                low[:, 0:8] = jnp.zeros((8, 8, 128), F32)
            else:
                up[...] += both[:, :, :128]
                low[:, 8:136] += both[:, :, 128:]
        out = (h0_ref, h1_ref)[a]
        for b in range(8):
            even = up[b, pl.ds(0, 64, stride=2)] + low[b, pl.ds(7, 64, stride=2)]
            odd = up[b, pl.ds(1, 64, stride=2)] + low[b, pl.ds(8, 64, stride=2)]
            out[b, :, 0:128] = jnp.maximum(even, 0.0).astype(BF16)
            out[b, :, 128:256] = jnp.maximum(odd, 0.0).astype(BF16)
        rows_ref[a] = out[7]


def first_layer(x, edge, rim, mine, theirs, seen):
    shape = jax.ShapeDtypeStruct((8, 64, 256), BF16)
    rows = jax.ShapeDtypeStruct((2, 64, 256), BF16)
    return pl.pallas_call(
        first_kernel,
        out_shape=(shape, shape, rows),
        in_specs=[SPEC] * 6,
        out_specs=(SPEC, SPEC, SPEC),
        scratch_shapes=[
            VMEM((256, 128), F32),
            VMEM((2, 128, 128), F32),
            VMEM((9, 256, 128), BF16),
            VMEM((8, 128, 128), F32),
            VMEM((8, 136, 128), F32),
        ],
        compiler_params=pltpu.CompilerParams(vmem_limit_bytes=24 * 2**20),
        cost_estimate=pl.CostEstimate(flops=2 * 2048 * 1152 * 256, bytes_accessed=4 * 2**20, transcendentals=0),
        name="first_layer",
    )(x, edge, rim, mine, theirs, seen)


def second_kernel(hm_ref, h0_ref, h1_ref, rows_ref, mine_ref, theirs_ref, stripe_ref, other_ref, out_ref, up, low):
    core, odd = lax.axis_index("depth") & 1, lax.axis_index("row") & 1

    def row(plane, at):
        if plane == 0:
            return hm_ref[at]
        return rows_ref[plane - 1] if at == 0 else (h0_ref, h1_ref)[plane - 1][at - 1]

    def weight(block):
        return block.astype(F32).reshape(256, 128).astype(BF16)

    def body(first, last, odd):
        low[:, :, 0:8] = jnp.zeros((2, 4, 8, 128), F32)

        def tap_of(t):
            if t == 13:
                return weight(last[0][:, 3])
            own, across = first if t < 13 else last
            place = t if t < 13 else t - 14
            if place == 0:
                return weight(own[:, 4])
            side, place = divmod(place - 1, 6)
            return weight(own[:, 5 + place] if side == odd else across[:, place])

        for tap in range(9):
            i, j = divmod(tap, 3)
            cells = jnp.concatenate([row(i, j + 2 * b) for b in range(4)], 0)
            k0, k1, k2 = (tap_of(3 * tap + k) for k in range(3))
            u = dot_t(cells, jnp.concatenate([k1, k2], 1))
            v = dot_t(cells[:, 128:], k0).reshape(4, 64, 256)
            for n in range(2):
                lanes = slice(128 * n, 128 * n + 128)
                if tap == 0:
                    up[n] = u[:, lanes]
                    low[n, :, 8:72] = v[:, :, lanes]
                else:
                    up[n] += u[:, lanes]
                    low[n, :, 8:72] += v[:, :, lanes]

    mine, theirs = (mine_ref, stripe_ref), (theirs_ref, other_ref)
    for c in range(2):
        for q in range(2):

            @pl.when(jnp.logical_and(core == c, odd == q))
            def _():
                body(*((mine, theirs) if c == 0 else (theirs, mine)), q)

    for b in range(4):
        for n in range(2):
            even = up[n, pl.ds(64 * b, 32, stride=2)] + low[n, b, pl.ds(7, 32, stride=2)]
            odd = up[n, pl.ds(64 * b + 1, 32, stride=2)] + low[n, b, pl.ds(8, 32, stride=2)]
            out_ref[0, b, :, 128 * n : 128 * n + 128] = jnp.maximum(even, 0.0).astype(BF16)
            out_ref[0, b, :, 256 + 128 * n : 384 + 128 * n] = jnp.maximum(odd, 0.0).astype(BF16)


def second_layer(hm, h0, h1, rows, mine, theirs, stripe, other):
    return pl.pallas_call(
        second_kernel,
        out_shape=jax.ShapeDtypeStruct((1, 4, 32, 512), BF16),
        in_specs=[SPEC] * 8,
        out_specs=SPEC,
        scratch_shapes=[VMEM((2, 256, 128), F32), VMEM((2, 4, 72, 128), F32)],
        compiler_params=pltpu.CompilerParams(vmem_limit_bytes=24 * 2**20),
        cost_estimate=pl.CostEstimate(flops=2 * 256 * 3456 * 256, bytes_accessed=3 * 2**20, transcendentals=0),
        name="second_layer",
    )(hm, h0, h1, rows, mine, theirs, stripe, other)


def pack_kernel(w1_hbm, w2_hbm, x_ref, send_ref, rim_ref, plane_ref, w1_ref, w2_ref, tiles, sems):
    weights = [
        pltpu.make_async_copy(w1_hbm, w1_ref, sems.at[2]),
        pltpu.make_async_copy(w2_hbm, w2_ref, sems.at[3]),
    ]
    copies = [
        pltpu.make_async_copy(x_ref.at[:, 15:16], rim_ref, sems.at[0]),
        pltpu.make_async_copy(x_ref.at[3:4], plane_ref, sems.at[1]),
    ]
    for copy in weights + copies:
        copy.start()
    odd = lax.axis_index("row") & 1
    for copy in weights:
        copy.wait()

    def tap(k, t):
        return w1_ref[t, k].astype(F32)

    def group(g):
        if g < 9:
            sides = [tap(1, g), tap(2, g)]
        else:
            t = 2 * (g - 9)
            sides = [tap(0, t), tap(0, t + 1) if t < 8 else jnp.zeros((4, 64), F32)]
        return jnp.concatenate(sides, 1)

    for m in range(7):
        tile = jnp.concatenate([group(2 * m), group(2 * m + 1)], 0).astype(BF16)
        tiles[m // 4, m % 4] = tile
    tiles[0, 4] = w2_ref[0]
    tiles[1, 3] = w2_ref[13]
    tiles[1, 4] = w2_ref[14]
    for half in range(2):
        for s in range(6):
            tiles[half, 5 + s] = w2_ref[14 * half + 1 + s + 6 * odd]
    for k in range(send_ref.shape[0] // 2):
        send_ref[2 * k : 2 * k + 2] = tiles[...]
    for copy in copies:
        copy.wait()


def pack(first, second, x, members):
    w1 = first.transpose(0, 1, 2, 4, 3).reshape(9, 3, 4, 64)
    w2 = second.transpose(0, 1, 2, 4, 3).reshape(27, 8, 128)
    shapes = ((members, 11, 8, 128), (4, 1, 128, 128), (1, 16, 128, 128))
    hbm = pl.BlockSpec(memory_space=pltpu.HBM)
    return pl.pallas_call(
        pack_kernel,
        out_shape=tuple(jax.ShapeDtypeStruct(shape, BF16) for shape in shapes),
        in_specs=[hbm, hbm, hbm],
        out_specs=(SPEC, SPEC, SPEC),
        scratch_shapes=[
            VMEM((9, 3, 4, 64), BF16),
            VMEM((27, 8, 128), BF16),
            VMEM((2, 11, 8, 128), BF16),
            pltpu.SemaphoreType.DMA((4,)),
        ],
        compiler_params=pltpu.CompilerParams(vmem_limit_bytes=60 * 2**20),
        name="pack",
    )(w1, w2, x)


def shift_by_one(x, axes, counts):
    if len(axes) == 1:
        pairs = [(i, i + 1) for i in range(counts[0] - 1)]
        return lax.ppermute(x, axes[0], pairs)
    n, m = counts
    pairs = [(i * m + j, (i + 1) * m + j + 1) for i in range(n - 1) for j in range(m - 1)]
    return lax.ppermute(x, axes, pairs)


def per_device(x, first_weight, second_weight):
    nd, nr = lax.axis_size("depth"), lax.axis_size("row")
    send, rim, plane = pack(first_weight, second_weight, x, nd)
    got = lax.all_to_all(send, "depth", 0, 0, tiled=False)

    edge = shift_by_one(plane, ("depth",), (nd,))
    corner = shift_by_one(plane[:, 15:], ("depth", "row"), (nd, nr))
    rim = shift_by_one(rim, ("row",), (nr,))
    rim = jnp.concatenate([corner, rim], 0)
    got, seen = lax.optimization_barrier((got, rim[0, 0, :16] + rim[1, 0, :16] + edge[0, 0, :16]))

    swaps = []
    for i in range(nd):
        for j in range(nr):
            base, at = j - j % 4, j % 4
            other = at ^ 1 if i % 2 == 0 else 3 - at
            swaps.append((i * nr + j, i * nr + base + other))
    stripe = lax.ppermute(got[:, 5:], ("depth", "row"), swaps)

    partners = [(i, i ^ 1) for i in range(nd)]
    theirs = lax.ppermute(got, "depth", partners)
    h0, h1, rows = first_layer(x, edge, rim, got, theirs, seen)
    rows = shift_by_one(rows, ("row",), (nr,))
    h0, stripe = lax.optimization_barrier((h0, stripe))
    hm = shift_by_one(jnp.concatenate([rows[1:], h1], 0), ("depth",), (nd,))
    other = lax.ppermute(stripe, "depth", partners)
    return second_layer(hm, h0, h1, rows, got, theirs, stripe, other)


def solution(mesh):
    return jax.shard_map(
        per_device,
        mesh=mesh,
        in_specs=(
            P("depth", "row", None, None),
            P(None, None, None, None, "depth"),
            P(None, None, None, None, "depth"),
        ),
        out_specs=P("depth", "row", None, None),
        check_vma=False,
    )
```

time: 77.9 us -> 69.6 us (0.89)
  the two profiles are of different devices: /device:TPU:392 before, /device:TPU:320 now
where the time goes in v2:
time: 69.6 us; the launch traced here: 69.1 us
  waiting for transfers between devices  30.7 us (44%)
  starting transfers between devices  30.4 us (44%)
  Pallas kernels  7.03 us (10%)
  local copies, waits for them, and re-layouts  0.8 us (1%)
    ppermute x1, waiting for transfers between devices, shift_by_one(): return lax.ppermute(x, axes, pairs)  16.6 us
    ppermute x4, waiting for transfers between devices, shift_by_one(): return lax.ppermute(x, axes[0], pairs)  13.3 us
    ppermute x4, starting transfers between devices, shift_by_one(): return lax.ppermute(x, axes[0], pairs)  11.3 us
    all_to_all x1, starting transfers between devices, per_device(): got = lax.all_to_all(send, 'depth', 0, 0, tiled=False)  8.74 us
    ppermute x1, starting transfers between devices, shift_by_one(): return lax.ppermute(x, axes, pairs)  4.14 us
    pallas_call x1, Pallas kernels, first_layer(): pl.pallas_call(first_kernel, out_shape=(shape, shape, rows), in_specs=[SP...  3.11 us
    ppermute x1, starting transfers between devices, per_device(): other = lax.ppermute(stripe, 'depth', partners)  2.46 us
    pallas_call x1, Pallas kernels, pack(): pl.pallas_call(pack_kernel, out_shape=tuple((jax.ShapeDtypeStruct(shape,...  2.42 us
  transfers between devices with their start and end apart: 9, of which 5 were waited for; matrix products, arithmetic and copies ran while one was open for 1% of the time, Pallas kernels for 4%

profile of v2, /device:TPU:320, one launch (start us, length us, event | category | flops | bytes accessed | tf_op | source)
XLA Modules:
  0.0 69.1 jit_solution(17212826981003943046)
XLA Ops:
  0.0 0.0 copy-start
  0.0 2.4 %pack.1 = (bf16[32,11,8,128]{3,2,1,0:T(8,128)(2,1)}, bf16[4,1,128,128]{3,2,1,0:T(8,128)(2,1)}, bf16[1,16,128,128]{3,2,1,0:T(8,128)(2,1)}) custom-call(bf16[9,3,4,64]{3,2,1,0:T(4,128)(2,1)} %bitcast.9, bf16[27,8,128]{2,1,0:T(8,128)(2,1)} %bitcast.8, bf16[4,16,128,128]{3,2,1,0:T(8,128)(2,1)} %x_ref.3), custom_call_target="tpu_custom_call" | custom-call | tf_op jit(solution)/shard_map/pack/pallas_call | solution.py:211
  2.4 8.7 %all-to-all-start = ((bf16[32,11,8,128]{3,2,1,0:T(8,128)(2,1)}), bf16[32,11,8,128]{3,2,1,0:T(8,128)(2,1)S(1)}, u32[]{:S(2)}, u32[]{:S(2)}) async-start(bf16[32,11,8,128]{3,2,1,0:T(8,128)(2,1)} %get-tuple-element.17), calls=%async_computation | async-start | bytes 1441792 | tf_op jit(solution)/shard_map/all_to_all | solution.py:239
  11.2 2.1 %collective-permute-start = (bf16[1,16,128,128]{3,2,1,0:T(8,128)(2,1)}, bf16[1,16,128,128]{3,2,1,0:T(8,128)(2,1)S(1)}, u32[]{:S(2)}, u32[]{:S(2)}) collective-permute-start(bf16[1,16,128,128]{3,2,1,0:T(8,128)(2,1)} %get-tuple-element.15), channel_id=1, source_target_pairs={{0,16},{16,32},{32,48},{48,64},{64,80},{80,96},{96,112},{112,128},... | collective-permute-start | bytes 1572872 | tf_op jit(solution)/shard_map/ppermute | solution.py:230
  13.2 3.4 %collective-permute-start.2 = (bf16[4,1,128,128]{3,2,1,0:T(8,128)(2,1)}, bf16[4,1,128,128]{3,2,1,0:T(8,128)(2,1)S(1)}, u32[]{:S(2)}, u32[]{:S(2)}) collective-permute-start(bf16[4,1,128,128]{3,2,1,0:T(8,128)(2,1)} %get-tuple-element.16), channel_id=1, source_target_pairs={{0,1},{1,2},{2,3},{3,4},{4,5},{5,6},{6,7},{7,8},{8,9},{9,10},{10,1... | collective-permute-start | bytes 393224 | tf_op jit(solution)/shard_map/ppermute | solution.py:230
  16.6 0.8 %slice.18 = bf16[1,1,128,128]{3,2,1,0:T(8,128)(2,1)S(1)} slice(bf16[1,16,128,128]{3,2,1,0:T(8,128)(2,1)} %get-tuple-element.15), slice={[0:1], [15:16], [0:128], [0:128]} | slice | bytes 65536 | tf_op jit(solution)/shard_map/slice | solution.py:242
  17.4 4.1 %collective-permute-start.1 = (bf16[1,1,128,128]{3,2,1,0:T(8,128)(2,1)S(1)}, bf16[1,1,128,128]{3,2,1,0:T(8,128)(2,1)S(1)}, u32[]{:S(2)}, u32[]{:S(2)}) collective-permute-start(bf16[1,1,128,128]{3,2,1,0:T(8,128)(2,1)S(1)} %slice.18), channel_id=1, source_target_pairs={{0,17},{1,18},{2,19},{3,20},{4,21},{5,22},{6,23},{7,24},{8,25},{9,... | collective-permute-start | bytes 98312 | tf_op jit(solution)/shard_map/ppermute | solution.py:233
  21.6 16.6 %collective-permute-done.1 = bf16[1,1,128,128]{3,2,1,0:T(8,128)(2,1)S(1)} collective-permute-done((bf16[1,1,128,128]{3,2,1,0:T(8,128)(2,1)S(1)}, bf16[1,1,128,128]{3,2,1,0:T(8,128)(2,1)S(1)}, u32[]{:S(2)}, u32[]{:S(2)}) %collective-permute-start.1) | collective-permute-done | bytes 32800 | tf_op jit(solution)/shard_map/ppermute | solution.py:233
  38.2 0.0 collective-permute-done.2
  38.2 0.0 collective-permute-done.edge_ref
  38.2 0.0 all-to-all-done.mine_ref
  38.2 1.9 %collective-permute-start.3 = (bf16[32,11,8,128]{3,2,1,0:T(8,128)(2,1)S(1)}, bf16[32,11,8,128]{3,2,1,0:T(8,128)(2,1)S(1)}, u32[]{:S(2)}, u32[]{:S(2)}) collective-permute-start(bf16[32,11,8,128]{3,2,1,0:T(8,128)(2,1)S(1)} %all-to-all-done.mine_ref), channel_id=1, source_target_pairs={{0,16},{16,0},{32,48},{48,32},{64,80},{80,64},{96,112},{112,96},{1... | collective-permute-start | bytes 2162696 | tf_op jit(solution)/shard_map/ppermute | solution.py:256
  40.1 1.9 %collective-permute-start.6 = (bf16[32,6,8,128]{3,2,1,0:T(8,128)(2,1)S(1)}, bf16[32,6,8,128]{3,2,1,0:T(8,128)(2,1)S(1)}, u32[]{:S(2)}, u32[]{:S(2)}) collective-permute-start(bf16[32,6,8,128]{3,2,1,0:T(8,128)(2,1)S(1)} %slice.23), channel_id=1, source_target_pairs={{0,1},{1,0},{2,3},{3,2},{4,5},{5,4},{6,7},{7,6},{8,9},{9,8},{10,11... | collective-permute-start | bytes 1179656 | tf_op jit(solution)/shard_map/ppermute | solution.py:253
  42.1 0.2 collective-permute-done.3.theirs_ref
  42.3 0.0 copy-done
  42.3 3.1 %first_layer.1 = (bf16[8,64,256]{2,1,0:T(8,128)(2,1)S(1)}, bf16[8,64,256]{2,1,0:T(8,128)(2,1)S(1)}, bf16[2,64,256]{2,1,0:T(8,128)(2,1)S(1)}) custom-call(bf16[4,16,128,128]{3,2,1,0:T(8,128)(2,1)S(1)} %copy-done, bf16[1,16,128,128]{3,2,1,0:T(8,128)(2,1)S(1)} %collective-permute-done.edge_ref, bf16[5,1,128,128]{3,2,1,0:T(8,128)(2,1)S(1)} %pad_maximum_fusion.1.rim_ref, ...), custom_call_target="tpu_custom_call" | custom-call | flops 1207959552 | bytes 4194304 | tf_op jit(solution)/shard_map/first_layer/pallas_call | solution.py:79
  45.4 3.8 %collective-permute-start.4 = (bf16[2,64,256]{2,1,0:T(8,128)(2,1)S(1)}, bf16[2,64,256]{2,1,0:T(8,128)(2,1)S(1)}, u32[]{:S(2)}, u32[]{:S(2)}) collective-permute-start(bf16[2,64,256]{2,1,0:T(8,128)(2,1)S(1)} %get-tuple-element.20), channel_id=1, source_target_pairs={{0,1},{1,2},{2,3},{3,4},{4,5},{5,6},{6,7},{7,8},{8,9},{9,10},{10,1... | collective-permute-start | bytes 196616 | tf_op jit(solution)/shard_map/ppermute | solution.py:230
  49.2 0.6 collective-permute-done.6.stripe_ref
  49.8 2.5 %collective-permute-start.7 = (bf16[32,6,8,128]{3,2,1,0:T(8,128)(2,1)S(1)}, bf16[32,6,8,128]{3,2,1,0:T(8,128)(2,1)S(1)}, u32[]{:S(2)}, u32[]{:S(2)}) collective-permute-start(bf16[32,6,8,128]{3,2,1,0:T(8,128)(2,1)S(1)} %collective-permute-done.6.stripe_ref), channel_id=1, source_target_pairs={{0,16},{16,0},{32,48},{48,32},{64,80},{80,64},{96,112},{112,96},{1... | collective-permute-start | bytes 1179656 | tf_op jit(solution)/shard_map/ppermute | solution.py:261
  52.3 5.2 %collective-permute-done.4.rows_ref = bf16[2,64,256]{2,1,0:T(8,128)(2,1)S(1)} collective-permute-done((bf16[2,64,256]{2,1,0:T(8,128)(2,1)S(1)}, bf16[2,64,256]{2,1,0:T(8,128)(2,1)S(1)}, u32[]{:S(2)}, u32[]{:S(2)}) %collective-permute-start.4) | collective-permute-done | bytes 65568 | tf_op jit(solution)/shard_map/ppermute | solution.py:230
  57.5 2.0 %collective-permute-start.5 = (bf16[9,64,256]{2,1,0:T(8,128)(2,1)S(1)}, bf16[9,64,256]{2,1,0:T(8,128)(2,1)S(1)}, u32[]{:S(2)}, u32[]{:S(2)}) collective-permute-start(bf16[9,64,256]{2,1,0:T(8,128)(2,1)S(1)} %pad_maximum_fusion), channel_id=1, source_target_pairs={{0,16},{16,32},{32,48},{48,64},{64,80},{80,96},{96,112},{112,128},... | collective-permute-start | bytes 884744 | tf_op jit(solution)/shard_map/ppermute | solution.py:230
  59.5 8.1 %collective-permute-done.5.hm_ref = bf16[9,64,256]{2,1,0:T(8,128)(2,1)S(1)} collective-permute-done((bf16[9,64,256]{2,1,0:T(8,128)(2,1)S(1)}, bf16[9,64,256]{2,1,0:T(8,128)(2,1)S(1)}, u32[]{:S(2)}, u32[]{:S(2)}) %collective-permute-start.5) | collective-permute-done | bytes 294944 | tf_op jit(solution)/shard_map/ppermute | solution.py:230
  67.6 0.0 collective-permute-done.7.other_ref
  67.6 1.5 %second_layer.1 = bf16[1,4,32,512]{3,2,1,0:T(8,128)(2,1)} custom-call(bf16[9,64,256]{2,1,0:T(8,128)(2,1)S(1)} %collective-permute-done.5.hm_ref, bf16[8,64,256]{2,1,0:T(8,128)(2,1)S(1)} %get-tuple-element.23.h0_ref, bf16[8,64,256]{2,1,0:T(8,128)(2,1)S(1)} %get-tuple-element.21.h1_ref, bf16[2,64,256]{2,1,0:T(8,128)(2,1)S(1)} %collective-permute-done.4.rows_ref, ...), custom_call_target="tpu_custom_call" | custom-call | flops 452984832 | bytes 3145728 | tf_op jit(solution)/shard_map/second_layer/pallas_call | solution.py:153
  (5 shorter events, 0.1 us)
Async XLA Ops:
  0.0 42.3 %copy-start = (bf16[4,16,128,128]{3,2,1,0:T(8,128)(2,1)S(1)}, bf16[4,16,128,128]{3,2,1,0:T(8,128)(2,1)}, u32[]{:S(2)}) copy-start(bf16[4,16,128,128]{3,2,1,0:T(8,128)(2,1)} %x_ref.3) | copy-start | bytes 6291460
  2.4 35.7 %all-to-all-start = ((bf16[32,11,8,128]{3,2,1,0:T(8,128)(2,1)}), bf16[32,11,8,128]{3,2,1,0:T(8,128)(2,1)S(1)}, u32[]{:S(2)}, u32[]{:S(2)}) async-start(bf16[32,11,8,128]{3,2,1,0:T(8,128)(2,1)} %get-tuple-element.17), calls=%async_computation | async-start | bytes 1441792 | tf_op jit(solution)/shard_map/all_to_all | solution.py:239
  11.2 27.0 %collective-permute-start = (bf16[1,16,128,128]{3,2,1,0:T(8,128)(2,1)}, bf16[1,16,128,128]{3,2,1,0:T(8,128)(2,1)S(1)}, u32[]{:S(2)}, u32[]{:S(2)}) collective-permute-start(bf16[1,16,128,128]{3,2,1,0:T(8,128)(2,1)} %get-tuple-element.15), channel_id=1, source_target_pairs={{0,16},{16,32},{32,48},{48,64},{64,80},{80,96},{96,112},{112,128},... | collective-permute-start | bytes 1572872 | tf_op jit(solution)/shard_map/ppermute | solution.py:230
  13.2 24.9 %collective-permute-start.2 = (bf16[4,1,128,128]{3,2,1,0:T(8,128)(2,1)}, bf16[4,1,128,128]{3,2,1,0:T(8,128)(2,1)S(1)}, u32[]{:S(2)}, u32[]{:S(2)}) collective-permute-start(bf16[4,1,128,128]{3,2,1,0:T(8,128)(2,1)} %get-tuple-element.16), channel_id=1, source_target_pairs={{0,1},{1,2},{2,3},{3,4},{4,5},{5,6},{6,7},{7,8},{8,9},{9,10},{10,1... | collective-permute-start | bytes 393224 | tf_op jit(solution)/shard_map/ppermute | solution.py:230
  17.4 20.7 %collective-permute-start.1 = (bf16[1,1,128,128]{3,2,1,0:T(8,128)(2,1)S(1)}, bf16[1,1,128,128]{3,2,1,0:T(8,128)(2,1)S(1)}, u32[]{:S(2)}, u32[]{:S(2)}) collective-permute-start(bf16[1,1,128,128]{3,2,1,0:T(8,128)(2,1)S(1)} %slice.18), channel_id=1, source_target_pairs={{0,17},{1,18},{2,19},{3,20},{4,21},{5,22},{6,23},{7,24},{8,25},{9,... | collective-permute-start | bytes 98312 | tf_op jit(solution)/shard_map/ppermute | solution.py:233
  38.2 4.1 %collective-permute-start.3 = (bf16[32,11,8,128]{3,2,1,0:T(8,128)(2,1)S(1)}, bf16[32,11,8,128]{3,2,1,0:T(8,128)(2,1)S(1)}, u32[]{:S(2)}, u32[]{:S(2)}) collective-permute-start(bf16[32,11,8,128]{3,2,1,0:T(8,128)(2,1)S(1)} %all-to-all-done.mine_ref), channel_id=1, source_target_pairs={{0,16},{16,0},{32,48},{48,32},{64,80},{80,64},{96,112},{112,96},{1... | collective-permute-start | bytes 2162696 | tf_op jit(solution)/shard_map/ppermute | solution.py:256
  40.1 9.7 %collective-permute-start.6 = (bf16[32,6,8,128]{3,2,1,0:T(8,128)(2,1)S(1)}, bf16[32,6,8,128]{3,2,1,0:T(8,128)(2,1)S(1)}, u32[]{:S(2)}, u32[]{:S(2)}) collective-permute-start(bf16[32,6,8,128]{3,2,1,0:T(8,128)(2,1)S(1)} %slice.23), channel_id=1, source_target_pairs={{0,1},{1,0},{2,3},{3,2},{4,5},{5,4},{6,7},{7,6},{8,9},{9,8},{10,11... | collective-permute-start | bytes 1179656 | tf_op jit(solution)/shard_map/ppermute | solution.py:253
  45.4 12.1 %collective-permute-start.4 = (bf16[2,64,256]{2,1,0:T(8,128)(2,1)S(1)}, bf16[2,64,256]{2,1,0:T(8,128)(2,1)S(1)}, u32[]{:S(2)}, u32[]{:S(2)}) collective-permute-start(bf16[2,64,256]{2,1,0:T(8,128)(2,1)S(1)} %get-tuple-element.20), channel_id=1, source_target_pairs={{0,1},{1,2},{2,3},{3,4},{4,5},{5,6},{6,7},{7,8},{8,9},{9,10},{10,1... | collective-permute-start | bytes 196616 | tf_op jit(solution)/shard_map/ppermute | solution.py:230
  49.8 17.8 %collective-permute-start.7 = (bf16[32,6,8,128]{3,2,1,0:T(8,128)(2,1)S(1)}, bf16[32,6,8,128]{3,2,1,0:T(8,128)(2,1)S(1)}, u32[]{:S(2)}, u32[]{:S(2)}) collective-permute-start(bf16[32,6,8,128]{3,2,1,0:T(8,128)(2,1)S(1)} %collective-permute-done.6.stripe_ref), channel_id=1, source_target_pairs={{0,16},{16,0},{32,48},{48,32},{64,80},{80,64},{96,112},{112,96},{1... | collective-permute-start | bytes 1179656 | tf_op jit(solution)/shard_map/ppermute | solution.py:261
  57.5 10.2 %collective-permute-start.5 = (bf16[9,64,256]{2,1,0:T(8,128)(2,1)S(1)}, bf16[9,64,256]{2,1,0:T(8,128)(2,1)S(1)}, u32[]{:S(2)}, u32[]{:S(2)}) collective-permute-start(bf16[9,64,256]{2,1,0:T(8,128)(2,1)S(1)} %pad_maximum_fusion), channel_id=1, source_target_pairs={{0,16},{16,32},{32,48},{48,64},{64,80},{80,96},{96,112},{112,128},... | collective-permute-start | bytes 884744 | tf_op jit(solution)/shard_map/ppermute | solution.py:230

commit v3 on v2

--- a/solution.py
+++ b/solution.py
@@ -8,6 +8,7 @@
 F32 = jnp.float32
 BF16 = jnp.bfloat16
 VMEM = pltpu.VMEM
+SENT = 13
 SPEC = pl.BlockSpec(memory_space=pltpu.VMEM)
 
 
@@ -15,10 +16,15 @@
     return lax.dot_general(a, b, (((1,), (1,)), ((), ())), preferred_element_type=F32)
 
 
-def first_kernel(x_ref, edge_ref, rim_ref, mine_ref, theirs_ref, seen_ref, h0_ref, h1_ref, rows_ref, stage, rows_up, weights, up, low):
+def first_kernel(x_ref, plane_ref, rim_ref, corner_ref, mine_ref, theirs_ref, seen_ref, h0_ref, h1_ref, stage, rows_up, weights, up, low):
     lanes = lax.broadcasted_iota(jnp.int32, (128, 128), 1)
     right = lanes >= 64
     core = lax.axis_index("depth") & 1
+
+    def put(tap, row, block):
+        i, j = divmod(tap, 3)
+        pair, side = (i, j - 1) if j else (3 + i // 2, i % 2)
+        weights[pair, row : row + 128, 128 * side : 128 * side + 128] = block.astype(BF16)
 
     def unpack(lower_ref, upper_ref):
         for tile in range(7):
@@ -29,12 +35,12 @@
                 group = 2 * tile + half
                 block = rows_up[half]
                 if group < 9:
-                    weights[group, 0:128] = block.astype(BF16)
+                    put(group, 0, block)
                 else:
                     tap = 2 * (group - 9)
-                    weights[tap, 128:256] = jnp.where(right, pltpu.roll(block, 64, 1), 0.0).astype(BF16)
+                    put(tap, 128, jnp.where(right, pltpu.roll(block, 64, 1), 0.0))
                     if tap + 1 < 9:
-                        weights[tap + 1, 128:256] = jnp.where(right, block, 0.0).astype(BF16)
+                        put(tap + 1, 128, jnp.where(right, block, 0.0))
 
     @pl.when(core == 0)
     def _():
@@ -45,62 +51,67 @@
         unpack(theirs_ref, mine_ref)
 
     def window(plane, j):
-        x = edge_ref[0] if plane == 0 else x_ref[plane - 1]
+        if plane == 0:
+            x, rim = plane_ref[0], corner_ref[0]
+        else:
+            x, rim = x_ref[plane - 1], rim_ref[plane - 1]
         x = x.reshape(8, 2, 128, 128)
         if j == 0:
-            x = jnp.concatenate([rim_ref[plane], x[0:7, 1]], 0)
+            parts = [rim[0:1], rim[2:3], x[0:7, 1]]
+        elif j == 1:
+            parts = [rim[1:2], x[:, 0]]
         else:
-            x = x[:, j - 1]
-        return x.reshape(1024, 128)
-
+            parts = [rim[2:3], x[:, 1]]
+        return jnp.concatenate(parts, 0).reshape(1152, 128)
+
+    h1_ref[9:] = jnp.zeros((SENT - 9, 64, 256), BF16)
     for a in range(2):
-        for tap in range(9):
-            i, j = divmod(tap, 3)
-            both = dot_t(window(2 * a + i, j), weights[tap]).reshape(8, 128, 256)
-            if tap == 0:
+        for pair in range(5):
+            if pair < 3:
+                cells = jnp.concatenate([window(2 * a + pair, 1), window(2 * a + pair, 2)], 1)
+            elif pair == 3:
+                cells = jnp.concatenate([window(2 * a, 0), window(2 * a + 1, 0)], 1)
+            else:
+                cells = window(2 * a + 2, 0)
+            both = dot_t(cells, weights[pair, :, : cells.shape[1]]).reshape(9, 128, 256)
+            if pair == 0:
                 up[...] = both[:, :, :128]
                 low[:, 8:136] = both[:, :, 128:]
-                low[:, 0:8] = jnp.zeros((8, 8, 128), F32)
+                low[:, 0:8] = jnp.zeros((9, 8, 128), F32)
             else:
                 up[...] += both[:, :, :128]
                 low[:, 8:136] += both[:, :, 128:]
         out = (h0_ref, h1_ref)[a]
-        for b in range(8):
+        for b in range(9):
             even = up[b, pl.ds(0, 64, stride=2)] + low[b, pl.ds(7, 64, stride=2)]
             odd = up[b, pl.ds(1, 64, stride=2)] + low[b, pl.ds(8, 64, stride=2)]
             out[b, :, 0:128] = jnp.maximum(even, 0.0).astype(BF16)
             out[b, :, 128:256] = jnp.maximum(odd, 0.0).astype(BF16)
-        rows_ref[a] = out[7]
-
-
-def first_layer(x, edge, rim, mine, theirs, seen):
-    shape = jax.ShapeDtypeStruct((8, 64, 256), BF16)
-    rows = jax.ShapeDtypeStruct((2, 64, 256), BF16)
+
+
+def first_layer(x, plane, rim, corner, mine, theirs, seen):
+    h0, h1 = (jax.ShapeDtypeStruct((n, 64, 256), BF16) for n in (9, SENT))
     return pl.pallas_call(
         first_kernel,
-        out_shape=(shape, shape, rows),
-        in_specs=[SPEC] * 6,
-        out_specs=(SPEC, SPEC, SPEC),
+        out_shape=(h0, h1),
+        in_specs=[SPEC] * 7,
+        out_specs=(SPEC, SPEC),
         scratch_shapes=[
             VMEM((256, 128), F32),
             VMEM((2, 128, 128), F32),
-            VMEM((9, 256, 128), BF16),
-            VMEM((8, 128, 128), F32),
-            VMEM((8, 136, 128), F32),
+            VMEM((5, 256, 256), BF16),
+            VMEM((9, 128, 128), F32),
+            VMEM((9, 136, 128), F32),
         ],
         compiler_params=pltpu.CompilerParams(vmem_limit_bytes=24 * 2**20),
-        cost_estimate=pl.CostEstimate(flops=2 * 2048 * 1152 * 256, bytes_accessed=4 * 2**20, transcendentals=0),
+        cost_estimate=pl.CostEstimate(flops=2 * 2304 * 1152 * 256, bytes_accessed=4 * 2**20, transcendentals=0),
         name="first_layer",
-    )(x, edge, rim, mine, theirs, seen)
-
-
-def second_kernel(hm_ref, h0_ref, h1_ref, rows_ref, mine_ref, theirs_ref, stripe_ref, other_ref, out_ref, up, low):
+    )(x, plane, rim, corner, mine, theirs, seen)
+
+
+def second_kernel(hm_ref, h0_ref, h1_ref, mine_ref, theirs_ref, stripe_ref, other_ref, out_ref, up, low):
     core, odd = lax.axis_index("depth") & 1, lax.axis_index("row") & 1
-
-    def row(plane, at):
-        if plane == 0:
-            return hm_ref[at]
-        return rows_ref[plane - 1] if at == 0 else (h0_ref, h1_ref)[plane - 1][at - 1]
+    planes = (hm_ref, h0_ref, h1_ref)
 
     def weight(block):
         return block.astype(F32).reshape(256, 128).astype(BF16)
@@ -120,7 +131,7 @@
 
         for tap in range(9):
             i, j = divmod(tap, 3)
-            cells = jnp.concatenate([row(i, j + 2 * b) for b in range(4)], 0)
+            cells = jnp.concatenate([planes[i][j + 2 * b] for b in range(4)], 0)
             k0, k1, k2 = (tap_of(3 * tap + k) for k in range(3))
             u = dot_t(cells, jnp.concatenate([k1, k2], 1))
             v = dot_t(cells[:, 128:], k0).reshape(4, 64, 256)
@@ -149,27 +160,28 @@
             out_ref[0, b, :, 256 + 128 * n : 384 + 128 * n] = jnp.maximum(odd, 0.0).astype(BF16)
 
 
-def second_layer(hm, h0, h1, rows, mine, theirs, stripe, other):
+def second_layer(hm, h0, h1, mine, theirs, stripe, other):
     return pl.pallas_call(
         second_kernel,
         out_shape=jax.ShapeDtypeStruct((1, 4, 32, 512), BF16),
-        in_specs=[SPEC] * 8,
+        in_specs=[SPEC] * 7,
         out_specs=SPEC,
         scratch_shapes=[VMEM((2, 256, 128), F32), VMEM((2, 4, 72, 128), F32)],
         compiler_params=pltpu.CompilerParams(vmem_limit_bytes=24 * 2**20),
         cost_estimate=pl.CostEstimate(flops=2 * 256 * 3456 * 256, bytes_accessed=3 * 2**20, transcendentals=0),
         name="second_layer",
-    )(hm, h0, h1, rows, mine, theirs, stripe, other)
-
-
-def pack_kernel(w1_hbm, w2_hbm, x_ref, send_ref, rim_ref, plane_ref, w1_ref, w2_ref, tiles, sems):
+    )(hm, h0, h1, mine, theirs, stripe, other)
+
+
+def pack_kernel(w1_hbm, w2_hbm, x_ref, send_ref, rim_ref, plane_ref, corner_ref, w1_ref, w2_ref, tiles, sems):
     weights = [
-        pltpu.make_async_copy(w1_hbm, w1_ref, sems.at[2]),
-        pltpu.make_async_copy(w2_hbm, w2_ref, sems.at[3]),
+        pltpu.make_async_copy(w1_hbm, w1_ref, sems.at[3]),
+        pltpu.make_async_copy(w2_hbm, w2_ref, sems.at[4]),
     ]
     copies = [
-        pltpu.make_async_copy(x_ref.at[:, 15:16], rim_ref, sems.at[0]),
+        pltpu.make_async_copy(x_ref.at[:, 13:16], rim_ref, sems.at[0]),
         pltpu.make_async_copy(x_ref.at[3:4], plane_ref, sems.at[1]),
+        pltpu.make_async_copy(x_ref.at[3:4, 13:16], corner_ref, sems.at[2]),
     ]
     for copy in weights + copies:
         copy.start()
@@ -206,18 +218,18 @@
 def pack(first, second, x, members):
     w1 = first.transpose(0, 1, 2, 4, 3).reshape(9, 3, 4, 64)
     w2 = second.transpose(0, 1, 2, 4, 3).reshape(27, 8, 128)
-    shapes = ((members, 11, 8, 128), (4, 1, 128, 128), (1, 16, 128, 128))
+    shapes = ((members, 11, 8, 128), (4, 3, 128, 128), (1, 16, 128, 128), (1, 3, 128, 128))
     hbm = pl.BlockSpec(memory_space=pltpu.HBM)
     return pl.pallas_call(
         pack_kernel,
         out_shape=tuple(jax.ShapeDtypeStruct(shape, BF16) for shape in shapes),
         in_specs=[hbm, hbm, hbm],
-        out_specs=(SPEC, SPEC, SPEC),
+        out_specs=(SPEC, SPEC, SPEC, SPEC),
         scratch_shapes=[
             VMEM((9, 3, 4, 64), BF16),
             VMEM((27, 8, 128), BF16),
             VMEM((2, 11, 8, 128), BF16),
-            pltpu.SemaphoreType.DMA((4,)),
+            pltpu.SemaphoreType.DMA((5,)),
         ],
         compiler_params=pltpu.CompilerParams(vmem_limit_bytes=60 * 2**20),
         name="pack",
@@ -233,16 +245,32 @@
     return lax.ppermute(x, axes, pairs)
 
 
+def glance_kernel(rim_ref, out_ref):
+    out_ref[...] = rim_ref[...]
+
+
+def glance(rim):
+    return pl.pallas_call(
+        glance_kernel,
+        out_shape=jax.ShapeDtypeStruct((16, 128), BF16),
+        in_specs=[SPEC],
+        out_specs=SPEC,
+        compiler_params=pltpu.CompilerParams(vmem_limit_bytes=2 * 2**20),
+        cost_estimate=pl.CostEstimate(flops=10**11, bytes_accessed=2**20, transcendentals=0),
+        name="glance",
+    )(rim)
+
+
 def per_device(x, first_weight, second_weight):
     nd, nr = lax.axis_size("depth"), lax.axis_size("row")
-    send, rim, plane = pack(first_weight, second_weight, x, nd)
+    send, rim, plane, corner = pack(first_weight, second_weight, x, nd)
     got = lax.all_to_all(send, "depth", 0, 0, tiled=False)
 
-    edge = shift_by_one(plane, ("depth",), (nd,))
-    corner = shift_by_one(plane[:, 15:], ("depth", "row"), (nd, nr))
     rim = shift_by_one(rim, ("row",), (nr,))
-    rim = jnp.concatenate([corner, rim], 0)
-    got, seen = lax.optimization_barrier((got, rim[0, 0, :16] + rim[1, 0, :16] + edge[0, 0, :16]))
+    plane = shift_by_one(plane, ("depth",), (nd,))
+    corner = shift_by_one(corner, ("depth", "row"), (nd, nr))
+    seen = glance(rim[0, 0, :16]) + plane[0, 0, :16] + corner[0, 0, :16]
+    got, seen = lax.optimization_barrier((got, seen))
 
     swaps = []
     for i in range(nd):
@@ -254,12 +282,12 @@
 
     partners = [(i, i ^ 1) for i in range(nd)]
     theirs = lax.ppermute(got, "depth", partners)
-    h0, h1, rows = first_layer(x, edge, rim, got, theirs, seen)
-    rows = shift_by_one(rows, ("row",), (nr,))
+    h0, h1 = first_layer(x, plane, rim, corner, got, theirs, seen)
+    hm = shift_by_one(h1, ("depth",), (nd,))
+
     h0, stripe = lax.optimization_barrier((h0, stripe))
-    hm = shift_by_one(jnp.concatenate([rows[1:], h1], 0), ("depth",), (nd,))
     other = lax.ppermute(stripe, "depth", partners)
-    return second_layer(hm, h0, h1, rows, got, theirs, stripe, other)
+    return second_layer(hm, h0, h1, got, theirs, stripe, other)
 
 
 def solution(mesh):

time: 69.6 us -> 66.3 us (0.953)
  the two profiles are of different devices: /device:TPU:320 before, /device:TPU:196 now
where the time goes in v3:
time: 66.3 us; the launch traced here: 65.8 us
  starting transfers between devices  30.1 us (45%)
  waiting for transfers between devices  27.5 us (41%)
  Pallas kernels  7.26 us (11%)
  other arithmetic  0.82 us (1%)
    all_to_all x1, waiting for transfers between devices, per_device(): got = lax.all_to_all(send, 'depth', 0, 0, tiled=False)  20.2 us
    all_to_all x1, starting transfers between devices, per_device(): got = lax.all_to_all(send, 'depth', 0, 0, tiled=False)  7.84 us
    ppermute x1, starting transfers between devices, shift_by_one(): return lax.ppermute(x, axes, pairs)  7.6 us
    ppermute x3, starting transfers between devices, shift_by_one(): return lax.ppermute(x, axes[0], pairs)  6.95 us
    ppermute x3, waiting for transfers between devices, shift_by_one(): return lax.ppermute(x, axes[0], pairs)  4.92 us
    ppermute x1, starting transfers between devices, per_device(): stripe = lax.ppermute(got[:, 5:], ('depth', 'row'), swaps)  3.4 us
    pallas_call x1, Pallas kernels, first_layer(): pl.pallas_call(first_kernel, out_shape=(h0, h1), in_specs=[SPEC] * 7, out...  3.31 us
    pallas_call x1, Pallas kernels, pack(): pl.pallas_call(pack_kernel, out_shape=tuple((jax.ShapeDtypeStruct(shape,...  2.44 us
  transfers between devices with their start and end apart: 8, of which 4 were waited for; matrix products, arithmetic and copies ran while one was open for 1% of the time, Pallas kernels for 5%

profile of v3, /device:TPU:196, one launch (start us, length us, event | category | flops | bytes accessed | tf_op | source)
XLA Modules:
  0.0 65.8 jit_solution(683330418571631282)
XLA Ops:
  0.0 2.4 %pack.1 = (bf16[32,11,8,128]{3,2,1,0:T(8,128)(2,1)}, bf16[4,3,128,128]{3,2,1,0:T(8,128)(2,1)}, bf16[1,16,128,128]{3,2,1,0:T(8,128)(2,1)}, bf16[1,3,128,128]{3,2,1,0:T(8,128)(2,1)}) custom-call(bf16[9,3,4,64]{3,2,1,0:T(4,128)(2,1)} %bitcast.19, bf16[27,8,128]{2,1,0:T(8,128)(2,1)} %bitcast.18, bf16[4,16,128,128]{3,2,1,0:T(8,128)(2,1)} %x_ref.3), custom_call_target="tpu_custom_call" | custom-call | tf_op jit(solution)/shard_map/pack/pallas_call | solution.py:223
  2.5 3.1 %collective-permute-start.1 = (bf16[4,3,128,128]{3,2,1,0:T(8,128)(2,1)}, bf16[4,3,128,128]{3,2,1,0:T(8,128)(2,1)S(1)}, u32[]{:S(2)}, u32[]{:S(2)}) collective-permute-start(bf16[4,3,128,128]{3,2,1,0:T(8,128)(2,1)} %get-tuple-element.16), channel_id=1, source_target_pairs={{0,1},{1,2},{2,3},{3,4},{4,5},{5,6},{6,7},{7,8},{8,9},{9,10},{10,1... | collective-permute-start | bytes 1179656 | tf_op jit(solution)/shard_map/ppermute | solution.py:242
  5.6 1.9 %collective-permute-start = (bf16[1,16,128,128]{3,2,1,0:T(8,128)(2,1)}, bf16[1,16,128,128]{3,2,1,0:T(8,128)(2,1)}, u32[]{:S(2)}, u32[]{:S(2)}) collective-permute-start(bf16[1,16,128,128]{3,2,1,0:T(8,128)(2,1)} %get-tuple-element.15), channel_id=1, source_target_pairs={{0,16},{16,32},{32,48},{48,64},{64,80},{80,96},{96,112},{112,128},... | collective-permute-start | bytes 1572872 | tf_op jit(solution)/shard_map/ppermute | solution.py:242
  7.5 7.6 %collective-permute-start.2 = (bf16[1,3,128,128]{3,2,1,0:T(8,128)(2,1)}, bf16[1,3,128,128]{3,2,1,0:T(8,128)(2,1)S(1)}, u32[]{:S(2)}, u32[]{:S(2)}) collective-permute-start(bf16[1,3,128,128]{3,2,1,0:T(8,128)(2,1)} %get-tuple-element.17), channel_id=1, source_target_pairs={{0,17},{1,18},{2,19},{3,20},{4,21},{5,22},{6,23},{7,24},{8,25},{9,... | collective-permute-start | bytes 294920 | tf_op jit(solution)/shard_map/ppermute | solution.py:245
  15.1 7.8 %all-to-all-start = ((bf16[32,11,8,128]{3,2,1,0:T(8,128)(2,1)}), bf16[32,11,8,128]{3,2,1,0:T(8,128)(2,1)S(1)}, u32[]{:S(2)}, u32[]{:S(2)}) async-start(bf16[32,11,8,128]{3,2,1,0:T(8,128)(2,1)} %get-tuple-element.18), calls=%async_computation | async-start | bytes 1441792 | tf_op jit(solution)/shard_map/all_to_all | solution.py:267
  22.9 0.0 collective-permute-done.1.rim_ref
  23.0 0.0 copy-start
  23.0 0.0 collective-permute-done.2.corner_ref
  23.0 0.0 collective-permute-done.plane_ref
  23.0 0.8 %fusion.seen_ref = bf16[16,128]{1,0:T(8,128)(2,1)S(1)} fusion(bf16[1,3,128,128]{3,2,1,0:T(8,128)(2,1)S(1)} %collective-permute-done.2.corner_ref, bf16[16,128]{1,0:T(8,128)(2,1)S(1)} %glance.1, bf16[1,16,128,128]{3,2,1,0:T(8,128)(2,1)} %collective-permute-done.plane_ref), kind=kLoop, calls=%fused_computation.1 | loop fusion | flops 4096 | bytes 16384 | tf_op jit(solution)/shard_map/add | solution.py:272
  23.8 20.2 %all-to-all-done.mine_ref = bf16[32,11,8,128]{3,2,1,0:T(8,128)(2,1)S(1)} async-done(((bf16[32,11,8,128]{3,2,1,0:T(8,128)(2,1)}), bf16[32,11,8,128]{3,2,1,0:T(8,128)(2,1)S(1)}, u32[]{:S(2)}, u32[]{:S(2)}) %all-to-all-start) | async-done | bytes 720928 | tf_op jit(solution)/shard_map/all_to_all | solution.py:267
  44.1 1.9 %collective-permute-start.3 = (bf16[32,11,8,128]{3,2,1,0:T(8,128)(2,1)S(1)}, bf16[32,11,8,128]{3,2,1,0:T(8,128)(2,1)S(1)}, u32[]{:S(2)}, u32[]{:S(2)}) collective-permute-start(bf16[32,11,8,128]{3,2,1,0:T(8,128)(2,1)S(1)} %all-to-all-done.mine_ref), channel_id=1, source_target_pairs={{0,16},{16,0},{32,48},{48,32},{64,80},{80,64},{96,112},{112,96},{1... | collective-permute-start | bytes 2162696 | tf_op jit(solution)/shard_map/ppermute | solution.py:284
  46.0 3.4 %collective-permute-start.5 = (bf16[32,6,8,128]{3,2,1,0:T(8,128)(2,1)S(1)}, bf16[32,6,8,128]{3,2,1,0:T(8,128)(2,1)S(1)}, u32[]{:S(2)}, u32[]{:S(2)}) collective-permute-start(bf16[32,6,8,128]{3,2,1,0:T(8,128)(2,1)S(1)} %slice.15), channel_id=1, source_target_pairs={{0,1},{1,0},{2,3},{3,2},{4,5},{5,4},{6,7},{7,6},{8,9},{9,8},{10,11... | collective-permute-start | bytes 1179656 | tf_op jit(solution)/shard_map/ppermute | solution.py:281
  49.4 0.0 collective-permute-done.3.theirs_ref
  49.4 0.0 copy-done
  49.4 3.3 %first_layer.1 = (bf16[9,64,256]{2,1,0:T(8,128)(2,1)S(1)}, bf16[13,64,256]{2,1,0:T(8,128)(2,1)S(1)}) custom-call(bf16[4,16,128,128]{3,2,1,0:T(8,128)(2,1)S(1)} %copy-done, bf16[1,16,128,128]{3,2,1,0:T(8,128)(2,1)} %collective-permute-done.plane_ref, bf16[4,3,128,128]{3,2,1,0:T(8,128)(2,1)S(1)} %collective-permute-done.1.rim_ref, ...), custom_call_target="tpu_custom_call" | custom-call | flops 1358954496 | bytes 4194304 | tf_op jit(solution)/shard_map/first_layer/pallas_call | solution.py:94
  52.8 1.9 %collective-permute-start.4 = (bf16[13,64,256]{2,1,0:T(8,128)(2,1)S(1)}, bf16[13,64,256]{2,1,0:T(8,128)(2,1)S(1)}, u32[]{:S(2)}, u32[]{:S(2)}) collective-permute-start(bf16[13,64,256]{2,1,0:T(8,128)(2,1)S(1)} %get-tuple-element.21.h1_ref), channel_id=1, source_target_pairs={{0,16},{16,32},{32,48},{48,64},{64,80},{80,96},{96,112},{112,128},... | collective-permute-start | bytes 1277960 | tf_op jit(solution)/shard_map/ppermute | solution.py:242
  54.7 1.0 %collective-permute-done.5.stripe_ref = bf16[32,6,8,128]{3,2,1,0:T(8,128)(2,1)S(1)} collective-permute-done((bf16[32,6,8,128]{3,2,1,0:T(8,128)(2,1)S(1)}, bf16[32,6,8,128]{3,2,1,0:T(8,128)(2,1)S(1)}, u32[]{:S(2)}, u32[]{:S(2)}) %collective-permute-start.5) | collective-permute-done | bytes 393248 | tf_op jit(solution)/shard_map/ppermute | solution.py:281
  55.7 2.4 %collective-permute-start.6 = (bf16[32,6,8,128]{3,2,1,0:T(8,128)(2,1)S(1)}, bf16[32,6,8,128]{3,2,1,0:T(8,128)(2,1)S(1)}, u32[]{:S(2)}, u32[]{:S(2)}) collective-permute-start(bf16[32,6,8,128]{3,2,1,0:T(8,128)(2,1)S(1)} %collective-permute-done.5.stripe_ref), channel_id=1, source_target_pairs={{0,16},{16,0},{32,48},{48,32},{64,80},{80,64},{96,112},{112,96},{1... | collective-permute-start | bytes 1179656 | tf_op jit(solution)/shard_map/ppermute | solution.py:289
  58.1 1.3 %collective-permute-done.6.other_ref = bf16[32,6,8,128]{3,2,1,0:T(8,128)(2,1)S(1)} collective-permute-done((bf16[32,6,8,128]{3,2,1,0:T(8,128)(2,1)S(1)}, bf16[32,6,8,128]{3,2,1,0:T(8,128)(2,1)S(1)}, u32[]{:S(2)}, u32[]{:S(2)}) %collective-permute-start.6) | collective-permute-done | bytes 393248 | tf_op jit(solution)/shard_map/ppermute | solution.py:289
  59.4 4.9 %collective-permute-done.4.hm_ref = bf16[13,64,256]{2,1,0:T(8,128)(2,1)S(1)} collective-permute-done((bf16[13,64,256]{2,1,0:T(8,128)(2,1)S(1)}, bf16[13,64,256]{2,1,0:T(8,128)(2,1)S(1)}, u32[]{:S(2)}, u32[]{:S(2)}) %collective-permute-start.4) | collective-permute-done | bytes 426016 | tf_op jit(solution)/shard_map/ppermute | solution.py:242
  64.3 1.5 %second_layer.1 = bf16[1,4,32,512]{3,2,1,0:T(8,128)(2,1)} custom-call(bf16[13,64,256]{2,1,0:T(8,128)(2,1)S(1)} %collective-permute-done.4.hm_ref, bf16[9,64,256]{2,1,0:T(8,128)(2,1)S(1)} %get-tuple-element.23.h0_ref, bf16[13,64,256]{2,1,0:T(8,128)(2,1)S(1)} %get-tuple-element.21.h1_ref, bf16[32,11,8,128]{3,2,1,0:T(8,128)(2,1)S(1)} %all-to-all-done.mine_ref, ...), custom_call_target="tpu_custom_call" | custom-call | flops 452984832 | bytes 3145728 | tf_op jit(solution)/shard_map/second_layer/pallas_call | solution.py:164
  (3 shorter events, 0.0 us)
Async XLA Ops:
  2.5 20.5 %collective-permute-start.1 = (bf16[4,3,128,128]{3,2,1,0:T(8,128)(2,1)}, bf16[4,3,128,128]{3,2,1,0:T(8,128)(2,1)S(1)}, u32[]{:S(2)}, u32[]{:S(2)}) collective-permute-start(bf16[4,3,128,128]{3,2,1,0:T(8,128)(2,1)} %get-tuple-element.16), channel_id=1, source_target_pairs={{0,1},{1,2},{2,3},{3,4},{4,5},{5,6},{6,7},{7,8},{8,9},{9,10},{10,1... | collective-permute-start | bytes 1179656 | tf_op jit(solution)/shard_map/ppermute | solution.py:242
  5.6 17.4 %collective-permute-start = (bf16[1,16,128,128]{3,2,1,0:T(8,128)(2,1)}, bf16[1,16,128,128]{3,2,1,0:T(8,128)(2,1)}, u32[]{:S(2)}, u32[]{:S(2)}) collective-permute-start(bf16[1,16,128,128]{3,2,1,0:T(8,128)(2,1)} %get-tuple-element.15), channel_id=1, source_target_pairs={{0,16},{16,32},{32,48},{48,64},{64,80},{80,96},{96,112},{112,128},... | collective-permute-start | bytes 1572872 | tf_op jit(solution)/shard_map/ppermute | solution.py:242
  7.5 15.5 %collective-permute-start.2 = (bf16[1,3,128,128]{3,2,1,0:T(8,128)(2,1)}, bf16[1,3,128,128]{3,2,1,0:T(8,128)(2,1)S(1)}, u32[]{:S(2)}, u32[]{:S(2)}) collective-permute-start(bf16[1,3,128,128]{3,2,1,0:T(8,128)(2,1)} %get-tuple-element.17), channel_id=1, source_target_pairs={{0,17},{1,18},{2,19},{3,20},{4,21},{5,22},{6,23},{7,24},{8,25},{9,... | collective-permute-start | bytes 294920 | tf_op jit(solution)/shard_map/ppermute | solution.py:245
  15.1 29.0 %all-to-all-start = ((bf16[32,11,8,128]{3,2,1,0:T(8,128)(2,1)}), bf16[32,11,8,128]{3,2,1,0:T(8,128)(2,1)S(1)}, u32[]{:S(2)}, u32[]{:S(2)}) async-start(bf16[32,11,8,128]{3,2,1,0:T(8,128)(2,1)} %get-tuple-element.18), calls=%async_computation | async-start | bytes 1441792 | tf_op jit(solution)/shard_map/all_to_all | solution.py:267
  23.0 26.5 %copy-start = (bf16[4,16,128,128]{3,2,1,0:T(8,128)(2,1)S(1)}, bf16[4,16,128,128]{3,2,1,0:T(8,128)(2,1)}, u32[]{:S(2)}) copy-start(bf16[4,16,128,128]{3,2,1,0:T(8,128)(2,1)} %x_ref.3) | copy-start | bytes 6291460
  44.1 5.4 %collective-permute-start.3 = (bf16[32,11,8,128]{3,2,1,0:T(8,128)(2,1)S(1)}, bf16[32,11,8,128]{3,2,1,0:T(8,128)(2,1)S(1)}, u32[]{:S(2)}, u32[]{:S(2)}) collective-permute-start(bf16[32,11,8,128]{3,2,1,0:T(8,128)(2,1)S(1)} %all-to-all-done.mine_ref), channel_id=1, source_target_pairs={{0,16},{16,0},{32,48},{48,32},{64,80},{80,64},{96,112},{112,96},{1... | collective-permute-start | bytes 2162696 | tf_op jit(solution)/shard_map/ppermute | solution.py:284
  46.0 9.7 %collective-permute-start.5 = (bf16[32,6,8,128]{3,2,1,0:T(8,128)(2,1)S(1)}, bf16[32,6,8,128]{3,2,1,0:T(8,128)(2,1)S(1)}, u32[]{:S(2)}, u32[]{:S(2)}) collective-permute-start(bf16[32,6,8,128]{3,2,1,0:T(8,128)(2,1)S(1)} %slice.15), channel_id=1, source_target_pairs={{0,1},{1,0},{2,3},{3,2},{4,5},{5,4},{6,7},{7,6},{8,9},{9,8},{10,11... | collective-permute-start | bytes 1179656 | tf_op jit(solution)/shard_map/ppermute | solution.py:281
  52.8 11.6 %collective-permute-start.4 = (bf16[13,64,256]{2,1,0:T(8,128)(2,1)S(1)}, bf16[13,64,256]{2,1,0:T(8,128)(2,1)S(1)}, u32[]{:S(2)}, u32[]{:S(2)}) collective-permute-start(bf16[13,64,256]{2,1,0:T(8,128)(2,1)S(1)} %get-tuple-element.21.h1_ref), channel_id=1, source_target_pairs={{0,16},{16,32},{32,48},{48,64},{64,80},{80,96},{96,112},{112,128},... | collective-permute-start | bytes 1277960 | tf_op jit(solution)/shard_map/ppermute | solution.py:242
  55.7 3.7 %collective-permute-start.6 = (bf16[32,6,8,128]{3,2,1,0:T(8,128)(2,1)S(1)}, bf16[32,6,8,128]{3,2,1,0:T(8,128)(2,1)S(1)}, u32[]{:S(2)}, u32[]{:S(2)}) collective-permute-start(bf16[32,6,8,128]{3,2,1,0:T(8,128)(2,1)S(1)} %collective-permute-done.5.stripe_ref), channel_id=1, source_target_pairs={{0,16},{16,0},{32,48},{48,32},{64,80},{80,64},{96,112},{112,96},{1... | collective-permute-start | bytes 1179656 | tf_op jit(solution)/shard_map/ppermute | solution.py:289

commit v4 on v3

--- a/solution.py
+++ b/solution.py
@@ -16,7 +16,43 @@
     return lax.dot_general(a, b, (((1,), (1,)), ((), ())), preferred_element_type=F32)
 
 
-def first_kernel(x_ref, plane_ref, rim_ref, corner_ref, mine_ref, theirs_ref, seen_ref, h0_ref, h1_ref, stage, rows_up, weights, up, low):
+def window(x, rim, j):
+    x = x.reshape(8, 2, 128, 128)
+    if j == 0:
+        parts = [rim[0:1], rim[2:3], x[0:7, 1]]
+    elif j == 1:
+        parts = [rim[1:2], x[:, 0]]
+    else:
+        parts = [rim[2:3], x[:, 1]]
+    return jnp.concatenate(parts, 0).reshape(1152, 128)
+
+
+def plane_of_hidden(cells, weights, out, up, low):
+    low[:, 0:8] = jnp.zeros((9, 8, 128), F32)
+    for pair in range(5):
+        if pair < 3:
+            left = jnp.concatenate([cells(pair, 1), cells(pair, 2)], 1)
+        elif pair == 3:
+            left = jnp.concatenate([cells(0, 0), cells(1, 0)], 1)
+        else:
+            left = cells(2, 0)
+        both = dot_t(left, weights[pair, :, : left.shape[1]]).reshape(9, 128, 256)
+        if pair == 0:
+            up[:, 0:128] = both[:, :, :128]
+            low[:, 8:136] = both[:, :, 128:]
+        else:
+            up[:, 0:128] += both[:, :, :128]
+            low[:, 8:136] += both[:, :, 128:]
+    for b in range(9):
+        even = up[b, pl.ds(0, 64, stride=2)] + low[b, pl.ds(7, 64, stride=2)]
+        odd = up[b, pl.ds(1, 64, stride=2)] + low[b, pl.ds(8, 64, stride=2)]
+        out[b, :, 0:128] = jnp.maximum(even, 0.0).astype(BF16)
+        out[b, :, 128:256] = jnp.maximum(odd, 0.0).astype(BF16)
+
+
+def last_kernel(x_ref, plane_hbm, rim_ref, mine_ref, theirs_ref, seen_ref, h1_ref, weights, plane_ref, stage, rows_up, up, low, sem):
+    fetch = pltpu.make_async_copy(plane_hbm, plane_ref, sem)
+    fetch.start()
     lanes = lax.broadcasted_iota(jnp.int32, (128, 128), 1)
     right = lanes >= 64
     core = lax.axis_index("depth") & 1
@@ -28,12 +64,12 @@
 
     def unpack(lower_ref, upper_ref):
         for tile in range(7):
-            stage[...] = (lower_ref, upper_ref)[tile // 4][:, tile % 4].astype(F32).reshape(256, 128)
+            stage[0:256] = (lower_ref, upper_ref)[tile // 4][:, tile % 4].astype(F32).reshape(256, 128)
             for r in range(8):
                 rows_up[r // 4, pl.ds(r % 4, 32, stride=4)] = stage[pl.ds(r, 32, stride=8)]
             for half in range(2):
                 group = 2 * tile + half
-                block = rows_up[half]
+                block = rows_up[half, 0:128]
                 if group < 9:
                     put(group, 0, block)
                 else:
@@ -50,63 +86,53 @@
     def _():
         unpack(theirs_ref, mine_ref)
 
-    def window(plane, j):
-        if plane == 0:
-            x, rim = plane_ref[0], corner_ref[0]
-        else:
-            x, rim = x_ref[plane - 1], rim_ref[plane - 1]
-        x = x.reshape(8, 2, 128, 128)
-        if j == 0:
-            parts = [rim[0:1], rim[2:3], x[0:7, 1]]
-        elif j == 1:
-            parts = [rim[1:2], x[:, 0]]
-        else:
-            parts = [rim[2:3], x[:, 1]]
-        return jnp.concatenate(parts, 0).reshape(1152, 128)
-
+    weights[4, :, 128:256] = jnp.zeros((256, 128), BF16)
     h1_ref[9:] = jnp.zeros((SENT - 9, 64, 256), BF16)
-    for a in range(2):
-        for pair in range(5):
-            if pair < 3:
-                cells = jnp.concatenate([window(2 * a + pair, 1), window(2 * a + pair, 2)], 1)
-            elif pair == 3:
-                cells = jnp.concatenate([window(2 * a, 0), window(2 * a + 1, 0)], 1)
-            else:
-                cells = window(2 * a + 2, 0)
-            both = dot_t(cells, weights[pair, :, : cells.shape[1]]).reshape(9, 128, 256)
-            if pair == 0:
-                up[...] = both[:, :, :128]
-                low[:, 8:136] = both[:, :, 128:]
-                low[:, 0:8] = jnp.zeros((9, 8, 128), F32)
-            else:
-                up[...] += both[:, :, :128]
-                low[:, 8:136] += both[:, :, 128:]
-        out = (h0_ref, h1_ref)[a]
-        for b in range(9):
-            even = up[b, pl.ds(0, 64, stride=2)] + low[b, pl.ds(7, 64, stride=2)]
-            odd = up[b, pl.ds(1, 64, stride=2)] + low[b, pl.ds(8, 64, stride=2)]
-            out[b, :, 0:128] = jnp.maximum(even, 0.0).astype(BF16)
-            out[b, :, 128:256] = jnp.maximum(odd, 0.0).astype(BF16)
-
-
-def first_layer(x, plane, rim, corner, mine, theirs, seen):
-    h0, h1 = (jax.ShapeDtypeStruct((n, 64, 256), BF16) for n in (9, SENT))
-    return pl.pallas_call(
-        first_kernel,
-        out_shape=(h0, h1),
-        in_specs=[SPEC] * 7,
-        out_specs=(SPEC, SPEC),
-        scratch_shapes=[
-            VMEM((256, 128), F32),
-            VMEM((2, 128, 128), F32),
-            VMEM((5, 256, 256), BF16),
-            VMEM((9, 128, 128), F32),
-            VMEM((9, 136, 128), F32),
-        ],
+
+    def cells(i, j):
+        return window(x_ref[1 + i], rim_ref[1 + i], j)
+
+    plane_of_hidden(cells, weights, h1_ref, up, low)
+    fetch.wait()
+
+
+def before_kernel(x_ref, plane_ref, rim_ref, corner_ref, weights, h0_ref, up, low):
+    def cells(i, j):
+        if i == 0:
+            return window(plane_ref[0], corner_ref[0], j)
+        return window(x_ref[i - 1], rim_ref[i - 1], j)
+
+    plane_of_hidden(cells, weights, h0_ref, up, low)
+
+
+SUMS = [VMEM((9, 136, 128), F32), VMEM((9, 136, 128), F32)]
+HIDDEN = jax.ShapeDtypeStruct((9, 64, 256), BF16)
+
+
+def last_hidden(x, plane, rim, mine, theirs, seen):
+    return pl.pallas_call(
+        last_kernel,
+        out_shape=(jax.ShapeDtypeStruct((SENT, 64, 256), BF16), jax.ShapeDtypeStruct((5, 256, 256), BF16), jax.ShapeDtypeStruct(plane.shape, BF16)),
+        in_specs=[SPEC, pl.BlockSpec(memory_space=pl.ANY)] + [SPEC] * 4,
+        out_specs=(SPEC, SPEC, SPEC),
+        scratch_shapes=[VMEM((264, 128), F32), VMEM((2, 136, 128), F32)] + SUMS + [pltpu.SemaphoreType.DMA(())],
         compiler_params=pltpu.CompilerParams(vmem_limit_bytes=24 * 2**20),
-        cost_estimate=pl.CostEstimate(flops=2 * 2304 * 1152 * 256, bytes_accessed=4 * 2**20, transcendentals=0),
-        name="first_layer",
-    )(x, plane, rim, corner, mine, theirs, seen)
+        cost_estimate=pl.CostEstimate(flops=2 * 1152 * 1152 * 256, bytes_accessed=2 * 2**20, transcendentals=0),
+        name="last_hidden",
+    )(x, plane, rim, mine, theirs, seen)
+
+
+def hidden_before(x, plane, rim, corner, weights):
+    return pl.pallas_call(
+        before_kernel,
+        out_shape=HIDDEN,
+        in_specs=[SPEC] * 5,
+        out_specs=SPEC,
+        scratch_shapes=SUMS,
+        compiler_params=pltpu.CompilerParams(vmem_limit_bytes=24 * 2**20),
+        cost_estimate=pl.CostEstimate(flops=2 * 1152 * 1152 * 256, bytes_accessed=2 * 2**20, transcendentals=0),
+        name="hidden_before",
+    )(x, plane, rim, corner, weights)
 
 
 def second_kernel(hm_ref, h0_ref, h1_ref, mine_ref, theirs_ref, stripe_ref, other_ref, out_ref, up, low):
@@ -138,10 +164,10 @@
             for n in range(2):
                 lanes = slice(128 * n, 128 * n + 128)
                 if tap == 0:
-                    up[n] = u[:, lanes]
+                    up[n, 0:256] = u[:, lanes]
                     low[n, :, 8:72] = v[:, :, lanes]
                 else:
-                    up[n] += u[:, lanes]
+                    up[n, 0:256] += u[:, lanes]
                     low[n, :, 8:72] += v[:, :, lanes]
 
     mine, theirs = (mine_ref, stripe_ref), (theirs_ref, other_ref)
@@ -166,7 +192,7 @@
         out_shape=jax.ShapeDtypeStruct((1, 4, 32, 512), BF16),
         in_specs=[SPEC] * 7,
         out_specs=SPEC,
-        scratch_shapes=[VMEM((2, 256, 128), F32), VMEM((2, 4, 72, 128), F32)],
+        scratch_shapes=[VMEM((2, 264, 128), F32), VMEM((2, 4, 72, 128), F32)],
         compiler_params=pltpu.CompilerParams(vmem_limit_bytes=24 * 2**20),
         cost_estimate=pl.CostEstimate(flops=2 * 256 * 3456 * 256, bytes_accessed=3 * 2**20, transcendentals=0),
         name="second_layer",
@@ -282,8 +308,9 @@
 
     partners = [(i, i ^ 1) for i in range(nd)]
     theirs = lax.ppermute(got, "depth", partners)
-    h0, h1 = first_layer(x, plane, rim, corner, got, theirs, seen)
+    h1, weights, plane = last_hidden(x, plane, rim, got, theirs, seen)
     hm = shift_by_one(h1, ("depth",), (nd,))
+    h0 = hidden_before(x, plane, rim, corner, weights)
 
     h0, stripe = lax.optimization_barrier((h0, stripe))
     other = lax.ppermute(stripe, "depth", partners)

time: 66.3 us -> 64.4 us (0.971)
  Pallas kernels: 7.26 us -> 6.54 us
    ppermute x3, waiting for transfers between devices: 4.92 us -> 3.24 us  [shift_by_one(): return lax.ppermute(x, axes[0], pairs)]
    pallas_call x1 -> x2, Pallas kernels: 3.31 us -> 2.6 us  [the longest x1 1.52 us: last_hidden(): pl.pallas_call(last_kernel, out_shape=(jax.ShapeDtypeStruct((SENT, 64, 25...]
    ppermute x1, waiting for transfers between devices: 0.99 us -> 1.7 us  [per_device(): stripe = lax.ppermute(got[:, 5:], ('depth', 'row'), swaps)]
  transfers between devices with their start and end apart: 8 -> 8, of which waited for: 4 -> 4; matrix products, arithmetic and copies ran while one was open for 1% -> 1% of each run, Pallas kernels for 5% -> 4%
where the time goes in v4:
time: 64.4 us; the launch traced here: 64 us
  starting transfers between devices  29.6 us (46%)
  waiting for transfers between devices  26.9 us (42%)
  Pallas kernels  6.54 us (10%)
  other arithmetic  0.82 us (1%)
    all_to_all x1, waiting for transfers between devices, per_device(): got = lax.all_to_all(send, 'depth', 0, 0, tiled=False)  20.2 us
    all_to_all x1, starting transfers between devices, per_device(): got = lax.all_to_all(send, 'depth', 0, 0, tiled=False)  7.84 us
    ppermute x1, starting transfers between devices, shift_by_one(): return lax.ppermute(x, axes, pairs)  7.6 us
    ppermute x3, starting transfers between devices, shift_by_one(): return lax.ppermute(x, axes[0], pairs)  6.95 us
    ppermute x1, starting transfers between devices, per_device(): stripe = lax.ppermute(got[:, 5:], ('depth', 'row'), swaps)  3.4 us
    ppermute x3, waiting for transfers between devices, shift_by_one(): return lax.ppermute(x, axes[0], pairs)  3.24 us
    pallas_call x1, Pallas kernels, pack(): pl.pallas_call(pack_kernel, out_shape=tuple((jax.ShapeDtypeStruct(shape,...  2.44 us
    ppermute x1, starting transfers between devices, per_device(): theirs = lax.ppermute(got, 'depth', partners)  1.91 us
  transfers between devices with their start and end apart: 8, of which 4 were waited for; matrix products, arithmetic and copies ran while one was open for 1% of the time, Pallas kernels for 4%

profile of v4, /device:TPU:196, one launch (start us, length us, event | category | flops | bytes accessed | tf_op | source)
XLA Modules:
  0.0 64.0 jit_solution(15045072363199549508)
XLA Ops:
  0.0 2.4 %pack.1 = (bf16[32,11,8,128]{3,2,1,0:T(8,128)(2,1)}, bf16[4,3,128,128]{3,2,1,0:T(8,128)(2,1)}, bf16[1,16,128,128]{3,2,1,0:T(8,128)(2,1)}, bf16[1,3,128,128]{3,2,1,0:T(8,128)(2,1)}) custom-call(bf16[9,3,4,64]{3,2,1,0:T(4,128)(2,1)} %bitcast.19, bf16[27,8,128]{2,1,0:T(8,128)(2,1)} %bitcast.18, bf16[4,16,128,128]{3,2,1,0:T(8,128)(2,1)} %x_ref.5), custom_call_target="tpu_custom_call" | custom-call | tf_op jit(solution)/shard_map/pack/pallas_call | solution.py:249
  2.5 3.1 %collective-permute-start.1 = (bf16[4,3,128,128]{3,2,1,0:T(8,128)(2,1)}, bf16[4,3,128,128]{3,2,1,0:T(8,128)(2,1)S(1)}, u32[]{:S(2)}, u32[]{:S(2)}) collective-permute-start(bf16[4,3,128,128]{3,2,1,0:T(8,128)(2,1)} %get-tuple-element.17), channel_id=1, source_target_pairs={{0,1},{1,2},{2,3},{3,4},{4,5},{5,6},{6,7},{7,8},{8,9},{9,10},{10,1... | collective-permute-start | bytes 1179656 | tf_op jit(solution)/shard_map/ppermute | solution.py:268
  5.6 1.9 %collective-permute-start = (bf16[1,16,128,128]{3,2,1,0:T(8,128)(2,1)}, bf16[1,16,128,128]{3,2,1,0:T(8,128)(2,1)}, u32[]{:S(2)}, u32[]{:S(2)}) collective-permute-start(bf16[1,16,128,128]{3,2,1,0:T(8,128)(2,1)} %get-tuple-element.16), channel_id=1, source_target_pairs={{0,16},{16,32},{32,48},{48,64},{64,80},{80,96},{96,112},{112,128},... | collective-permute-start | bytes 1572872 | tf_op jit(solution)/shard_map/ppermute | solution.py:268
  7.5 7.6 %collective-permute-start.2 = (bf16[1,3,128,128]{3,2,1,0:T(8,128)(2,1)}, bf16[1,3,128,128]{3,2,1,0:T(8,128)(2,1)S(1)}, u32[]{:S(2)}, u32[]{:S(2)}) collective-permute-start(bf16[1,3,128,128]{3,2,1,0:T(8,128)(2,1)} %get-tuple-element.19), channel_id=1, source_target_pairs={{0,17},{1,18},{2,19},{3,20},{4,21},{5,22},{6,23},{7,24},{8,25},{9,... | collective-permute-start | bytes 294920 | tf_op jit(solution)/shard_map/ppermute | solution.py:271
  15.1 7.8 %all-to-all-start = ((bf16[32,11,8,128]{3,2,1,0:T(8,128)(2,1)}), bf16[32,11,8,128]{3,2,1,0:T(8,128)(2,1)S(1)}, u32[]{:S(2)}, u32[]{:S(2)}) async-start(bf16[32,11,8,128]{3,2,1,0:T(8,128)(2,1)} %get-tuple-element.18), calls=%async_computation | async-start | bytes 1441792 | tf_op jit(solution)/shard_map/all_to_all | solution.py:293
  22.9 0.0 collective-permute-done.1.rim_ref
  23.0 0.0 copy-start
  23.0 0.0 collective-permute-done.2.corner_ref
  23.0 0.0 collective-permute-done.plane_hbm
  23.0 0.8 %fusion.seen_ref = bf16[16,128]{1,0:T(8,128)(2,1)S(1)} fusion(bf16[1,3,128,128]{3,2,1,0:T(8,128)(2,1)S(1)} %collective-permute-done.2.corner_ref, bf16[16,128]{1,0:T(8,128)(2,1)S(1)} %glance.1, bf16[1,16,128,128]{3,2,1,0:T(8,128)(2,1)} %collective-permute-done.plane_hbm), kind=kLoop, calls=%fused_computation.1 | loop fusion | flops 4096 | bytes 16384 | tf_op jit(solution)/shard_map/add | solution.py:298
  23.8 20.2 %all-to-all-done.mine_ref = bf16[32,11,8,128]{3,2,1,0:T(8,128)(2,1)S(1)} async-done(((bf16[32,11,8,128]{3,2,1,0:T(8,128)(2,1)}), bf16[32,11,8,128]{3,2,1,0:T(8,128)(2,1)S(1)}, u32[]{:S(2)}, u32[]{:S(2)}) %all-to-all-start) | async-done | bytes 720928 | tf_op jit(solution)/shard_map/all_to_all | solution.py:293
  44.1 1.9 %collective-permute-start.3 = (bf16[32,11,8,128]{3,2,1,0:T(8,128)(2,1)S(1)}, bf16[32,11,8,128]{3,2,1,0:T(8,128)(2,1)S(1)}, u32[]{:S(2)}, u32[]{:S(2)}) collective-permute-start(bf16[32,11,8,128]{3,2,1,0:T(8,128)(2,1)S(1)} %all-to-all-done.mine_ref), channel_id=1, source_target_pairs={{0,16},{16,0},{32,48},{48,32},{64,80},{80,64},{96,112},{112,96},{1... | collective-permute-start | bytes 2162696 | tf_op jit(solution)/shard_map/ppermute | solution.py:310
  46.0 3.4 %collective-permute-start.5 = (bf16[32,6,8,128]{3,2,1,0:T(8,128)(2,1)S(1)}, bf16[32,6,8,128]{3,2,1,0:T(8,128)(2,1)S(1)}, u32[]{:S(2)}, u32[]{:S(2)}) collective-permute-start(bf16[32,6,8,128]{3,2,1,0:T(8,128)(2,1)S(1)} %slice.15), channel_id=1, source_target_pairs={{0,1},{1,0},{2,3},{3,2},{4,5},{5,4},{6,7},{7,6},{8,9},{9,8},{10,11... | collective-permute-start | bytes 1179656 | tf_op jit(solution)/shard_map/ppermute | solution.py:307
  49.4 0.0 collective-permute-done.3.theirs_ref
  49.4 0.0 copy-done
  49.4 1.5 %last_hidden.1 = (bf16[13,64,256]{2,1,0:T(8,128)(2,1)S(1)}, bf16[5,256,256]{2,1,0:T(8,128)(2,1)S(1)}, bf16[1,16,128,128]{3,2,1,0:T(8,128)(2,1)S(1)}) custom-call(bf16[4,16,128,128]{3,2,1,0:T(8,128)(2,1)S(1)} %copy-done, bf16[1,16,128,128]{3,2,1,0:T(8,128)(2,1)} %collective-permute-done.plane_hbm, ...), custom_call_target="tpu_custom_call" | custom-call | flops 679477248 | bytes 2097152 | tf_op jit(solution)/shard_map/last_hidden/pallas_call | solution.py:113
  51.0 1.9 %collective-permute-start.4 = (bf16[13,64,256]{2,1,0:T(8,128)(2,1)S(1)}, bf16[13,64,256]{2,1,0:T(8,128)(2,1)S(1)}, u32[]{:S(2)}, u32[]{:S(2)}) collective-permute-start(bf16[13,64,256]{2,1,0:T(8,128)(2,1)S(1)} %get-tuple-element.22.h1_ref), channel_id=1, source_target_pairs={{0,16},{16,32},{32,48},{48,64},{64,80},{80,96},{96,112},{112,128},... | collective-permute-start | bytes 1277960 | tf_op jit(solution)/shard_map/ppermute | solution.py:268
  52.9 1.1 %hidden_before.1.h0_ref = bf16[9,64,256]{2,1,0:T(8,128)(2,1)S(1)} custom-call(bf16[4,16,128,128]{3,2,1,0:T(8,128)(2,1)S(1)} %copy-done, bf16[1,16,128,128]{3,2,1,0:T(8,128)(2,1)S(1)} %get-tuple-element.23.plane_ref, bf16[4,3,128,128]{3,2,1,0:T(8,128)(2,1)S(1)} %collective-permute-done.1.rim_ref, ...), custom_call_target="tpu_custom_call" | custom-call | flops 679477248 | bytes 2097152 | tf_op jit(solution)/shard_map/hidden_before/pallas_call | solution.py:126
  54.0 1.7 %collective-permute-done.5.stripe_ref = bf16[32,6,8,128]{3,2,1,0:T(8,128)(2,1)S(1)} collective-permute-done((bf16[32,6,8,128]{3,2,1,0:T(8,128)(2,1)S(1)}, bf16[32,6,8,128]{3,2,1,0:T(8,128)(2,1)S(1)}, u32[]{:S(2)}, u32[]{:S(2)}) %collective-permute-start.5) | collective-permute-done | bytes 393248 | tf_op jit(solution)/shard_map/ppermute | solution.py:307
  55.7 1.9 %collective-permute-start.6 = (bf16[32,6,8,128]{3,2,1,0:T(8,128)(2,1)S(1)}, bf16[32,6,8,128]{3,2,1,0:T(8,128)(2,1)S(1)}, u32[]{:S(2)}, u32[]{:S(2)}) collective-permute-start(bf16[32,6,8,128]{3,2,1,0:T(8,128)(2,1)S(1)} %collective-permute-done.5.stripe_ref), channel_id=1, source_target_pairs={{0,16},{16,0},{32,48},{48,32},{64,80},{80,64},{96,112},{112,96},{1... | collective-permute-start | bytes 1179656 | tf_op jit(solution)/shard_map/ppermute | solution.py:316
  57.6 1.7 %collective-permute-done.6.other_ref = bf16[32,6,8,128]{3,2,1,0:T(8,128)(2,1)S(1)} collective-permute-done((bf16[32,6,8,128]{3,2,1,0:T(8,128)(2,1)S(1)}, bf16[32,6,8,128]{3,2,1,0:T(8,128)(2,1)S(1)}, u32[]{:S(2)}, u32[]{:S(2)}) %collective-permute-start.6) | collective-permute-done | bytes 393248 | tf_op jit(solution)/shard_map/ppermute | solution.py:316
  59.3 3.2 %collective-permute-done.4.hm_ref = bf16[13,64,256]{2,1,0:T(8,128)(2,1)S(1)} collective-permute-done((bf16[13,64,256]{2,1,0:T(8,128)(2,1)S(1)}, bf16[13,64,256]{2,1,0:T(8,128)(2,1)S(1)}, u32[]{:S(2)}, u32[]{:S(2)}) %collective-permute-start.4) | collective-permute-done | bytes 426016 | tf_op jit(solution)/shard_map/ppermute | solution.py:268
  62.5 1.5 %second_layer.1 = bf16[1,4,32,512]{3,2,1,0:T(8,128)(2,1)} custom-call(bf16[13,64,256]{2,1,0:T(8,128)(2,1)S(1)} %collective-permute-done.4.hm_ref, bf16[9,64,256]{2,1,0:T(8,128)(2,1)S(1)} %hidden_before.1.h0_ref, bf16[13,64,256]{2,1,0:T(8,128)(2,1)S(1)} %get-tuple-element.22.h1_ref, bf16[32,11,8,128]{3,2,1,0:T(8,128)(2,1)S(1)} %all-to-all-done.mine_ref, ...), custom_call_target="tpu_custom_call" | custom-call | flops 452984832 | bytes 3145728 | tf_op jit(solution)/shard_map/second_layer/pallas_call | solution.py:190
  (3 shorter events, 0.0 us)
Async XLA Ops:
  2.5 20.5 %collective-permute-start.1 = (bf16[4,3,128,128]{3,2,1,0:T(8,128)(2,1)}, bf16[4,3,128,128]{3,2,1,0:T(8,128)(2,1)S(1)}, u32[]{:S(2)}, u32[]{:S(2)}) collective-permute-start(bf16[4,3,128,128]{3,2,1,0:T(8,128)(2,1)} %get-tuple-element.17), channel_id=1, source_target_pairs={{0,1},{1,2},{2,3},{3,4},{4,5},{5,6},{6,7},{7,8},{8,9},{9,10},{10,1... | collective-permute-start | bytes 1179656 | tf_op jit(solution)/shard_map/ppermute | solution.py:268
  5.6 17.4 %collective-permute-start = (bf16[1,16,128,128]{3,2,1,0:T(8,128)(2,1)}, bf16[1,16,128,128]{3,2,1,0:T(8,128)(2,1)}, u32[]{:S(2)}, u32[]{:S(2)}) collective-permute-start(bf16[1,16,128,128]{3,2,1,0:T(8,128)(2,1)} %get-tuple-element.16), channel_id=1, source_target_pairs={{0,16},{16,32},{32,48},{48,64},{64,80},{80,96},{96,112},{112,128},... | collective-permute-start | bytes 1572872 | tf_op jit(solution)/shard_map/ppermute | solution.py:268
  7.5 15.5 %collective-permute-start.2 = (bf16[1,3,128,128]{3,2,1,0:T(8,128)(2,1)}, bf16[1,3,128,128]{3,2,1,0:T(8,128)(2,1)S(1)}, u32[]{:S(2)}, u32[]{:S(2)}) collective-permute-start(bf16[1,3,128,128]{3,2,1,0:T(8,128)(2,1)} %get-tuple-element.19), channel_id=1, source_target_pairs={{0,17},{1,18},{2,19},{3,20},{4,21},{5,22},{6,23},{7,24},{8,25},{9,... | collective-permute-start | bytes 294920 | tf_op jit(solution)/shard_map/ppermute | solution.py:271
  15.1 29.0 %all-to-all-start = ((bf16[32,11,8,128]{3,2,1,0:T(8,128)(2,1)}), bf16[32,11,8,128]{3,2,1,0:T(8,128)(2,1)S(1)}, u32[]{:S(2)}, u32[]{:S(2)}) async-start(bf16[32,11,8,128]{3,2,1,0:T(8,128)(2,1)} %get-tuple-element.18), calls=%async_computation | async-start | bytes 1441792 | tf_op jit(solution)/shard_map/all_to_all | solution.py:293
  23.0 26.5 %copy-start = (bf16[4,16,128,128]{3,2,1,0:T(8,128)(2,1)S(1)}, bf16[4,16,128,128]{3,2,1,0:T(8,128)(2,1)}, u32[]{:S(2)}) copy-start(bf16[4,16,128,128]{3,2,1,0:T(8,128)(2,1)} %x_ref.5) | copy-start | bytes 6291460
  44.1 5.4 %collective-permute-start.3 = (bf16[32,11,8,128]{3,2,1,0:T(8,128)(2,1)S(1)}, bf16[32,11,8,128]{3,2,1,0:T(8,128)(2,1)S(1)}, u32[]{:S(2)}, u32[]{:S(2)}) collective-permute-start(bf16[32,11,8,128]{3,2,1,0:T(8,128)(2,1)S(1)} %all-to-all-done.mine_ref), channel_id=1, source_target_pairs={{0,16},{16,0},{32,48},{48,32},{64,80},{80,64},{96,112},{112,96},{1... | collective-permute-start | bytes 2162696 | tf_op jit(solution)/shard_map/ppermute | solution.py:310
  46.0 9.7 %collective-permute-start.5 = (bf16[32,6,8,128]{3,2,1,0:T(8,128)(2,1)S(1)}, bf16[32,6,8,128]{3,2,1,0:T(8,128)(2,1)S(1)}, u32[]{:S(2)}, u32[]{:S(2)}) collective-permute-start(bf16[32,6,8,128]{3,2,1,0:T(8,128)(2,1)S(1)} %slice.15), channel_id=1, source_target_pairs={{0,1},{1,0},{2,3},{3,2},{4,5},{5,4},{6,7},{7,6},{8,9},{9,8},{10,11... | collective-permute-start | bytes 1179656 | tf_op jit(solution)/shard_map/ppermute | solution.py:307
  51.0 11.6 %collective-permute-start.4 = (bf16[13,64,256]{2,1,0:T(8,128)(2,1)S(1)}, bf16[13,64,256]{2,1,0:T(8,128)(2,1)S(1)}, u32[]{:S(2)}, u32[]{:S(2)}) collective-permute-start(bf16[13,64,256]{2,1,0:T(8,128)(2,1)S(1)} %get-tuple-element.22.h1_ref), channel_id=1, source_target_pairs={{0,16},{16,32},{32,48},{48,64},{64,80},{80,96},{96,112},{112,128},... | collective-permute-start | bytes 1277960 | tf_op jit(solution)/shard_map/ppermute | solution.py:268
  55.7 3.6 %collective-permute-start.6 = (bf16[32,6,8,128]{3,2,1,0:T(8,128)(2,1)S(1)}, bf16[32,6,8,128]{3,2,1,0:T(8,128)(2,1)S(1)}, u32[]{:S(2)}, u32[]{:S(2)}) collective-permute-start(bf16[32,6,8,128]{3,2,1,0:T(8,128)(2,1)S(1)} %collective-permute-done.5.stripe_ref), channel_id=1, source_target_pairs={{0,16},{16,0},{32,48},{48,32},{64,80},{80,64},{96,112},{112,96},{1... | collective-permute-start | bytes 1179656 | tf_op jit(solution)/shard_map/ppermute | solution.py:316

commit v5 on v4

--- a/solution.py
+++ b/solution.py
@@ -199,15 +199,14 @@
     )(hm, h0, h1, mine, theirs, stripe, other)
 
 
-def pack_kernel(w1_hbm, w2_hbm, x_ref, send_ref, rim_ref, plane_ref, corner_ref, w1_ref, w2_ref, tiles, sems):
+def pack_kernel(w1_hbm, w2_hbm, x_ref, send_ref, rim_ref, plane_ref, corner_ref, w1_ref, w2_ref, tiles, rim, plane, sems, out_sems):
     weights = [
         pltpu.make_async_copy(w1_hbm, w1_ref, sems.at[3]),
         pltpu.make_async_copy(w2_hbm, w2_ref, sems.at[4]),
     ]
     copies = [
-        pltpu.make_async_copy(x_ref.at[:, 13:16], rim_ref, sems.at[0]),
-        pltpu.make_async_copy(x_ref.at[3:4], plane_ref, sems.at[1]),
-        pltpu.make_async_copy(x_ref.at[3:4, 13:16], corner_ref, sems.at[2]),
+        pltpu.make_async_copy(x_ref.at[:, 13:16], rim, sems.at[0]),
+        pltpu.make_async_copy(x_ref.at[3:4], plane, sems.at[1]),
     ]
     for copy in weights + copies:
         copy.start()
@@ -235,9 +234,22 @@
     for half in range(2):
         for s in range(6):
             tiles[half, 5 + s] = w2_ref[14 * half + 1 + s + 6 * odd]
-    for k in range(send_ref.shape[0] // 2):
-        send_ref[2 * k : 2 * k + 2] = tiles[...]
+    outs = [
+        pltpu.make_async_copy(tiles, send_ref.at[2 * k : 2 * k + 2], out_sems.at[k])
+        for k in range(send_ref.shape[0] // 2)
+    ]
+    edges = [
+        pltpu.make_async_copy(rim, rim_ref, sems.at[2]),
+        pltpu.make_async_copy(plane, plane_ref, sems.at[5]),
+        pltpu.make_async_copy(plane.at[:, 13:16], corner_ref, sems.at[6]),
+    ]
+    for copy in outs:
+        copy.start()
     for copy in copies:
+        copy.wait()
+    for copy in edges:
+        copy.start()
+    for copy in edges + outs:
         copy.wait()
 
 
@@ -250,12 +262,15 @@
         pack_kernel,
         out_shape=tuple(jax.ShapeDtypeStruct(shape, BF16) for shape in shapes),
         in_specs=[hbm, hbm, hbm],
-        out_specs=(SPEC, SPEC, SPEC, SPEC),
+        out_specs=(hbm, hbm, hbm, hbm),
         scratch_shapes=[
             VMEM((9, 3, 4, 64), BF16),
             VMEM((27, 8, 128), BF16),
             VMEM((2, 11, 8, 128), BF16),
-            pltpu.SemaphoreType.DMA((5,)),
+            VMEM((4, 3, 128, 128), BF16),
+            VMEM((1, 16, 128, 128), BF16),
+            pltpu.SemaphoreType.DMA((7,)),
+            pltpu.SemaphoreType.DMA((members // 2,)),
         ],
         compiler_params=pltpu.CompilerParams(vmem_limit_bytes=60 * 2**20),
         name="pack",

time: 64.4 us -> 64.4 us (level)
  no operation moved by 1% of the time
where the time goes in v5:
time: 64.4 us; the launch traced here: 64 us
  starting transfers between devices  29.6 us (46%)
  waiting for transfers between devices  26.9 us (42%)
  Pallas kernels  6.48 us (10%)
  other arithmetic  0.82 us (1%)
    all_to_all x1, waiting for transfers between devices, per_device(): got = lax.all_to_all(send, 'depth', 0, 0, tiled=False)  20.2 us
    all_to_all x1, starting transfers between devices, per_device(): got = lax.all_to_all(send, 'depth', 0, 0, tiled=False)  7.84 us
    ppermute x1, starting transfers between devices, shift_by_one(): return lax.ppermute(x, axes, pairs)  7.6 us
    ppermute x3, starting transfers between devices, shift_by_one(): return lax.ppermute(x, axes[0], pairs)  6.95 us
    ppermute x1, starting transfers between devices, per_device(): stripe = lax.ppermute(got[:, 5:], ('depth', 'row'), swaps)  3.4 us
    ppermute x3, waiting for transfers between devices, shift_by_one(): return lax.ppermute(x, axes[0], pairs)  3.24 us
    pallas_call x1, Pallas kernels, pack(): pl.pallas_call(pack_kernel, out_shape=tuple((jax.ShapeDtypeStruct(shape,...  2.38 us
    ppermute x1, starting transfers between devices, per_device(): theirs = lax.ppermute(got, 'depth', partners)  1.91 us
  transfers between devices with their start and end apart: 8, of which 4 were waited for; matrix products, arithmetic and copies ran while one was open for 1% of the time, Pallas kernels for 4%

profile of v5, /device:TPU:196, one launch (start us, length us, event | category | flops | bytes accessed | tf_op | source)
XLA Modules:
  0.0 64.0 jit_solution(16560628246600962778)
XLA Ops:
  0.0 2.4 %pack.1 = (bf16[32,11,8,128]{3,2,1,0:T(8,128)(2,1)}, bf16[4,3,128,128]{3,2,1,0:T(8,128)(2,1)}, bf16[1,16,128,128]{3,2,1,0:T(8,128)(2,1)}, bf16[1,3,128,128]{3,2,1,0:T(8,128)(2,1)}) custom-call(bf16[9,3,4,64]{3,2,1,0:T(4,128)(2,1)} %bitcast.19, bf16[27,8,128]{2,1,0:T(8,128)(2,1)} %bitcast.18, bf16[4,16,128,128]{3,2,1,0:T(8,128)(2,1)} %x_ref.5), custom_call_target="tpu_custom_call" | custom-call | tf_op jit(solution)/shard_map/pack/pallas_call | solution.py:261
  2.4 3.1 %collective-permute-start.1 = (bf16[4,3,128,128]{3,2,1,0:T(8,128)(2,1)}, bf16[4,3,128,128]{3,2,1,0:T(8,128)(2,1)S(1)}, u32[]{:S(2)}, u32[]{:S(2)}) collective-permute-start(bf16[4,3,128,128]{3,2,1,0:T(8,128)(2,1)} %get-tuple-element.17), channel_id=1, source_target_pairs={{0,1},{1,2},{2,3},{3,4},{4,5},{5,6},{6,7},{7,8},{8,9},{9,10},{10,1... | collective-permute-start | bytes 1179656 | tf_op jit(solution)/shard_map/ppermute | solution.py:283
  5.5 1.9 %collective-permute-start = (bf16[1,16,128,128]{3,2,1,0:T(8,128)(2,1)}, bf16[1,16,128,128]{3,2,1,0:T(8,128)(2,1)}, u32[]{:S(2)}, u32[]{:S(2)}) collective-permute-start(bf16[1,16,128,128]{3,2,1,0:T(8,128)(2,1)} %get-tuple-element.16), channel_id=1, source_target_pairs={{0,16},{16,32},{32,48},{48,64},{64,80},{80,96},{96,112},{112,128},... | collective-permute-start | bytes 1572872 | tf_op jit(solution)/shard_map/ppermute | solution.py:283
  7.4 7.6 %collective-permute-start.2 = (bf16[1,3,128,128]{3,2,1,0:T(8,128)(2,1)}, bf16[1,3,128,128]{3,2,1,0:T(8,128)(2,1)S(1)}, u32[]{:S(2)}, u32[]{:S(2)}) collective-permute-start(bf16[1,3,128,128]{3,2,1,0:T(8,128)(2,1)} %get-tuple-element.19), channel_id=1, source_target_pairs={{0,17},{1,18},{2,19},{3,20},{4,21},{5,22},{6,23},{7,24},{8,25},{9,... | collective-permute-start | bytes 294920 | tf_op jit(solution)/shard_map/ppermute | solution.py:286
  15.0 7.8 %all-to-all-start = ((bf16[32,11,8,128]{3,2,1,0:T(8,128)(2,1)}), bf16[32,11,8,128]{3,2,1,0:T(8,128)(2,1)S(1)}, u32[]{:S(2)}, u32[]{:S(2)}) async-start(bf16[32,11,8,128]{3,2,1,0:T(8,128)(2,1)} %get-tuple-element.18), calls=%async_computation | async-start | bytes 1441792 | tf_op jit(solution)/shard_map/all_to_all | solution.py:308
  22.9 0.0 collective-permute-done.1.rim_ref
  22.9 0.0 copy-start
  22.9 0.0 collective-permute-done.2.corner_ref
  22.9 0.0 collective-permute-done.plane_hbm
  22.9 0.8 %fusion.seen_ref = bf16[16,128]{1,0:T(8,128)(2,1)S(1)} fusion(bf16[1,3,128,128]{3,2,1,0:T(8,128)(2,1)S(1)} %collective-permute-done.2.corner_ref, bf16[16,128]{1,0:T(8,128)(2,1)S(1)} %glance.1, bf16[1,16,128,128]{3,2,1,0:T(8,128)(2,1)} %collective-permute-done.plane_hbm), kind=kLoop, calls=%fused_computation.1 | loop fusion | flops 4096 | bytes 16384 | tf_op jit(solution)/shard_map/add | solution.py:313
  23.8 20.2 %all-to-all-done.mine_ref = bf16[32,11,8,128]{3,2,1,0:T(8,128)(2,1)S(1)} async-done(((bf16[32,11,8,128]{3,2,1,0:T(8,128)(2,1)}), bf16[32,11,8,128]{3,2,1,0:T(8,128)(2,1)S(1)}, u32[]{:S(2)}, u32[]{:S(2)}) %all-to-all-start) | async-done | bytes 720928 | tf_op jit(solution)/shard_map/all_to_all | solution.py:308
  44.0 1.9 %collective-permute-start.3 = (bf16[32,11,8,128]{3,2,1,0:T(8,128)(2,1)S(1)}, bf16[32,11,8,128]{3,2,1,0:T(8,128)(2,1)S(1)}, u32[]{:S(2)}, u32[]{:S(2)}) collective-permute-start(bf16[32,11,8,128]{3,2,1,0:T(8,128)(2,1)S(1)} %all-to-all-done.mine_ref), channel_id=1, source_target_pairs={{0,16},{16,0},{32,48},{48,32},{64,80},{80,64},{96,112},{112,96},{1... | collective-permute-start | bytes 2162696 | tf_op jit(solution)/shard_map/ppermute | solution.py:325
  46.0 3.4 %collective-permute-start.5 = (bf16[32,6,8,128]{3,2,1,0:T(8,128)(2,1)S(1)}, bf16[32,6,8,128]{3,2,1,0:T(8,128)(2,1)S(1)}, u32[]{:S(2)}, u32[]{:S(2)}) collective-permute-start(bf16[32,6,8,128]{3,2,1,0:T(8,128)(2,1)S(1)} %slice.15), channel_id=1, source_target_pairs={{0,1},{1,0},{2,3},{3,2},{4,5},{5,4},{6,7},{7,6},{8,9},{9,8},{10,11... | collective-permute-start | bytes 1179656 | tf_op jit(solution)/shard_map/ppermute | solution.py:322
  49.4 0.0 collective-permute-done.3.theirs_ref
  49.4 0.0 copy-done
  49.4 1.5 %last_hidden.1 = (bf16[13,64,256]{2,1,0:T(8,128)(2,1)S(1)}, bf16[5,256,256]{2,1,0:T(8,128)(2,1)S(1)}, bf16[1,16,128,128]{3,2,1,0:T(8,128)(2,1)S(1)}) custom-call(bf16[4,16,128,128]{3,2,1,0:T(8,128)(2,1)S(1)} %copy-done, bf16[1,16,128,128]{3,2,1,0:T(8,128)(2,1)} %collective-permute-done.plane_hbm, ...), custom_call_target="tpu_custom_call" | custom-call | flops 679477248 | bytes 2097152 | tf_op jit(solution)/shard_map/last_hidden/pallas_call | solution.py:113
  50.9 1.9 %collective-permute-start.4 = (bf16[13,64,256]{2,1,0:T(8,128)(2,1)S(1)}, bf16[13,64,256]{2,1,0:T(8,128)(2,1)S(1)}, u32[]{:S(2)}, u32[]{:S(2)}) collective-permute-start(bf16[13,64,256]{2,1,0:T(8,128)(2,1)S(1)} %get-tuple-element.22.h1_ref), channel_id=1, source_target_pairs={{0,16},{16,32},{32,48},{48,64},{64,80},{80,96},{96,112},{112,128},... | collective-permute-start | bytes 1277960 | tf_op jit(solution)/shard_map/ppermute | solution.py:283
  52.8 1.1 %hidden_before.1.h0_ref = bf16[9,64,256]{2,1,0:T(8,128)(2,1)S(1)} custom-call(bf16[4,16,128,128]{3,2,1,0:T(8,128)(2,1)S(1)} %copy-done, bf16[1,16,128,128]{3,2,1,0:T(8,128)(2,1)S(1)} %get-tuple-element.23.plane_ref, bf16[4,3,128,128]{3,2,1,0:T(8,128)(2,1)S(1)} %collective-permute-done.1.rim_ref, ...), custom_call_target="tpu_custom_call" | custom-call | flops 679477248 | bytes 2097152 | tf_op jit(solution)/shard_map/hidden_before/pallas_call | solution.py:126
  53.9 1.7 %collective-permute-done.5.stripe_ref = bf16[32,6,8,128]{3,2,1,0:T(8,128)(2,1)S(1)} collective-permute-done((bf16[32,6,8,128]{3,2,1,0:T(8,128)(2,1)S(1)}, bf16[32,6,8,128]{3,2,1,0:T(8,128)(2,1)S(1)}, u32[]{:S(2)}, u32[]{:S(2)}) %collective-permute-start.5) | collective-permute-done | bytes 393248 | tf_op jit(solution)/shard_map/ppermute | solution.py:322
  55.6 1.9 %collective-permute-start.6 = (bf16[32,6,8,128]{3,2,1,0:T(8,128)(2,1)S(1)}, bf16[32,6,8,128]{3,2,1,0:T(8,128)(2,1)S(1)}, u32[]{:S(2)}, u32[]{:S(2)}) collective-permute-start(bf16[32,6,8,128]{3,2,1,0:T(8,128)(2,1)S(1)} %collective-permute-done.5.stripe_ref), channel_id=1, source_target_pairs={{0,16},{16,0},{32,48},{48,32},{64,80},{80,64},{96,112},{112,96},{1... | collective-permute-start | bytes 1179656 | tf_op jit(solution)/shard_map/ppermute | solution.py:331
  57.5 1.7 %collective-permute-done.6.other_ref = bf16[32,6,8,128]{3,2,1,0:T(8,128)(2,1)S(1)} collective-permute-done((bf16[32,6,8,128]{3,2,1,0:T(8,128)(2,1)S(1)}, bf16[32,6,8,128]{3,2,1,0:T(8,128)(2,1)S(1)}, u32[]{:S(2)}, u32[]{:S(2)}) %collective-permute-start.6) | collective-permute-done | bytes 393248 | tf_op jit(solution)/shard_map/ppermute | solution.py:331
  59.2 3.2 %collective-permute-done.4.hm_ref = bf16[13,64,256]{2,1,0:T(8,128)(2,1)S(1)} collective-permute-done((bf16[13,64,256]{2,1,0:T(8,128)(2,1)S(1)}, bf16[13,64,256]{2,1,0:T(8,128)(2,1)S(1)}, u32[]{:S(2)}, u32[]{:S(2)}) %collective-permute-start.4) | collective-permute-done | bytes 426016 | tf_op jit(solution)/shard_map/ppermute | solution.py:283
  62.5 1.5 %second_layer.1 = bf16[1,4,32,512]{3,2,1,0:T(8,128)(2,1)} custom-call(bf16[13,64,256]{2,1,0:T(8,128)(2,1)S(1)} %collective-permute-done.4.hm_ref, bf16[9,64,256]{2,1,0:T(8,128)(2,1)S(1)} %hidden_before.1.h0_ref, bf16[13,64,256]{2,1,0:T(8,128)(2,1)S(1)} %get-tuple-element.22.h1_ref, bf16[32,11,8,128]{3,2,1,0:T(8,128)(2,1)S(1)} %all-to-all-done.mine_ref, ...), custom_call_target="tpu_custom_call" | custom-call | flops 452984832 | bytes 3145728 | tf_op jit(solution)/shard_map/second_layer/pallas_call | solution.py:190
  (3 shorter events, 0.0 us)
Async XLA Ops:
  2.4 20.5 %collective-permute-start.1 = (bf16[4,3,128,128]{3,2,1,0:T(8,128)(2,1)}, bf16[4,3,128,128]{3,2,1,0:T(8,128)(2,1)S(1)}, u32[]{:S(2)}, u32[]{:S(2)}) collective-permute-start(bf16[4,3,128,128]{3,2,1,0:T(8,128)(2,1)} %get-tuple-element.17), channel_id=1, source_target_pairs={{0,1},{1,2},{2,3},{3,4},{4,5},{5,6},{6,7},{7,8},{8,9},{9,10},{10,1... | collective-permute-start | bytes 1179656 | tf_op jit(solution)/shard_map/ppermute | solution.py:283
  5.5 17.4 %collective-permute-start = (bf16[1,16,128,128]{3,2,1,0:T(8,128)(2,1)}, bf16[1,16,128,128]{3,2,1,0:T(8,128)(2,1)}, u32[]{:S(2)}, u32[]{:S(2)}) collective-permute-start(bf16[1,16,128,128]{3,2,1,0:T(8,128)(2,1)} %get-tuple-element.16), channel_id=1, source_target_pairs={{0,16},{16,32},{32,48},{48,64},{64,80},{80,96},{96,112},{112,128},... | collective-permute-start | bytes 1572872 | tf_op jit(solution)/shard_map/ppermute | solution.py:283
  7.4 15.5 %collective-permute-start.2 = (bf16[1,3,128,128]{3,2,1,0:T(8,128)(2,1)}, bf16[1,3,128,128]{3,2,1,0:T(8,128)(2,1)S(1)}, u32[]{:S(2)}, u32[]{:S(2)}) collective-permute-start(bf16[1,3,128,128]{3,2,1,0:T(8,128)(2,1)} %get-tuple-element.19), channel_id=1, source_target_pairs={{0,17},{1,18},{2,19},{3,20},{4,21},{5,22},{6,23},{7,24},{8,25},{9,... | collective-permute-start | bytes 294920 | tf_op jit(solution)/shard_map/ppermute | solution.py:286
  15.0 29.0 %all-to-all-start = ((bf16[32,11,8,128]{3,2,1,0:T(8,128)(2,1)}), bf16[32,11,8,128]{3,2,1,0:T(8,128)(2,1)S(1)}, u32[]{:S(2)}, u32[]{:S(2)}) async-start(bf16[32,11,8,128]{3,2,1,0:T(8,128)(2,1)} %get-tuple-element.18), calls=%async_computation | async-start | bytes 1441792 | tf_op jit(solution)/shard_map/all_to_all | solution.py:308
  22.9 26.5 %copy-start = (bf16[4,16,128,128]{3,2,1,0:T(8,128)(2,1)S(1)}, bf16[4,16,128,128]{3,2,1,0:T(8,128)(2,1)}, u32[]{:S(2)}) copy-start(bf16[4,16,128,128]{3,2,1,0:T(8,128)(2,1)} %x_ref.5) | copy-start | bytes 6291460
  44.0 5.4 %collective-permute-start.3 = (bf16[32,11,8,128]{3,2,1,0:T(8,128)(2,1)S(1)}, bf16[32,11,8,128]{3,2,1,0:T(8,128)(2,1)S(1)}, u32[]{:S(2)}, u32[]{:S(2)}) collective-permute-start(bf16[32,11,8,128]{3,2,1,0:T(8,128)(2,1)S(1)} %all-to-all-done.mine_ref), channel_id=1, source_target_pairs={{0,16},{16,0},{32,48},{48,32},{64,80},{80,64},{96,112},{112,96},{1... | collective-permute-start | bytes 2162696 | tf_op jit(solution)/shard_map/ppermute | solution.py:325
  46.0 9.7 %collective-permute-start.5 = (bf16[32,6,8,128]{3,2,1,0:T(8,128)(2,1)S(1)}, bf16[32,6,8,128]{3,2,1,0:T(8,128)(2,1)S(1)}, u32[]{:S(2)}, u32[]{:S(2)}) collective-permute-start(bf16[32,6,8,128]{3,2,1,0:T(8,128)(2,1)S(1)} %slice.15), channel_id=1, source_target_pairs={{0,1},{1,0},{2,3},{3,2},{4,5},{5,4},{6,7},{7,6},{8,9},{9,8},{10,11... | collective-permute-start | bytes 1179656 | tf_op jit(solution)/shard_map/ppermute | solution.py:322
  50.9 11.6 %collective-permute-start.4 = (bf16[13,64,256]{2,1,0:T(8,128)(2,1)S(1)}, bf16[13,64,256]{2,1,0:T(8,128)(2,1)S(1)}, u32[]{:S(2)}, u32[]{:S(2)}) collective-permute-start(bf16[13,64,256]{2,1,0:T(8,128)(2,1)S(1)} %get-tuple-element.22.h1_ref), channel_id=1, source_target_pairs={{0,16},{16,32},{32,48},{48,64},{64,80},{80,96},{96,112},{112,128},... | collective-permute-start | bytes 1277960 | tf_op jit(solution)/shard_map/ppermute | solution.py:283
  55.6 3.6 %collective-permute-start.6 = (bf16[32,6,8,128]{3,2,1,0:T(8,128)(2,1)S(1)}, bf16[32,6,8,128]{3,2,1,0:T(8,128)(2,1)S(1)}, u32[]{:S(2)}, u32[]{:S(2)}) collective-permute-start(bf16[32,6,8,128]{3,2,1,0:T(8,128)(2,1)S(1)} %collective-permute-done.5.stripe_ref), channel_id=1, source_target_pairs={{0,16},{16,0},{32,48},{48,32},{64,80},{80,64},{96,112},{112,96},{1... | collective-permute-start | bytes 1179656 | tf_op jit(solution)/shard_map/ppermute | solution.py:331
